TPU v7x, 256 devices: a whole 4x4x8 slice. The times are simulated.
256 devices in a mesh: clip: 16 (over x, y), tile: 16 (over z, core).
Axes of the slice: x: 4, y: 4, z: 8, core: 2. Of those that a mesh axis runs over, the one named last changes fastest.
Arguments:
- decoder_input: bfloat16 [16, 16, 32, 96, 128], P('clip', 'tile'), may hold values from -210 to 210
- reward_grad: bfloat16 [16, 32, 32, 96, 128], P('clip', 'tile'), may hold values from -6 to 6
- reward_owner: int32 [16, 16, 1], P('clip'), may hold values from 0 to 15; in each aligned block of 16 rows (0 to 15, 16 to 31, ..., all dimensions but the last counted through in order) at most 2 rows name the same one
- scored_frame: int32 [16, 16], P('clip'), may hold values from 0 to 15
- first_gain: float32 [96], replicated, may hold values from 0.1 to 1.9
- second_gain: float32 [96], replicated, may hold values from 0.1 to 1.9
- first_kernel: bfloat16 [3, 3, 3, 96, 96], replicated, may hold values from -0.125 to 0.125
- second_kernel: bfloat16 [3, 3, 3, 96, 96], replicated, may hold values from -0.125 to 0.125
Outputs:
- feature_grad: bfloat16 [16, 16, 32, 96, 128], P('clip', 'tile')
- first_kernel_grad: float32 [3, 3, 3, 96, 96], replicated
- second_kernel_grad: float32 [3, 3, 3, 96, 96], replicated
Inputs may be any that keep to these rules, and one draw needn't show every extreme that they name: `reward_owner`: in each clip at most 2 scored entries share a reward device, and in every draw some device of some clip holds exactly 2; every slot that no entry names is ignored.
All inputs are finite; a program needn't handle non-finite values.
Results may differ from a plain program's by a relative error of at most 0.0073.
Values may be sent and summed in bfloat16 or wider, within the bound.
A program may use at most 128 MiB of HBM per device.

v0:
```python
import math

import jax
import jax.numpy as jnp
from jax import lax
from jax.sharding import PartitionSpec as P

epsilon = 1e-06


def with_halo(block, sides, width):
    for axis, dim in sides:
        count = lax.axis_size(axis)
        forward = [(i, i + 1) for i in range(count - 1)]
        backward = [(target, source) for source, target in forward]
        low = lax.ppermute(
            lax.slice_in_dim(block, block.shape[dim] - width, None, axis=dim), axis, forward
        )
        high = lax.ppermute(lax.slice_in_dim(block, 0, width, axis=dim), axis, backward)
        block = jnp.concatenate([low, block, high], axis=dim)
    return block


def slot_table(owners, scored, device_count, slot_count, frames):
    onehot = (owners[:, None] == jnp.arange(device_count, dtype=jnp.int32)[None, :]).astype(
        jnp.int32
    )
    before = jnp.cumsum(onehot, axis=0) - onehot
    ranking = jnp.sum(before * onehot, axis=1)
    position = owners * slot_count + ranking
    by_frame = (scored[None, :] == jnp.arange(frames, dtype=jnp.int32)[:, None]).astype(jnp.float32)
    by_slot = (
        position[:, None] == jnp.arange(device_count * slot_count, dtype=jnp.int32)[None, :]
    ).astype(jnp.float32)
    return jnp.dot(by_frame, by_slot, preferred_element_type=jnp.float32)


def conv_forward(padded_rows, kernel):
    result = lax.conv_general_dilated(
        padded_rows[None],
        kernel,
        window_strides=(1, 1, 1),
        padding=((2, 0), (0, 0), (1, 1)),
        dimension_numbers=("NDHCW", "DHWOI", "NDHCW"),
        preferred_element_type=jnp.float32,
    )
    return result[0]


def conv_input_grad(padded_rows, kernel):
    flipped = kernel[::-1, ::-1, ::-1]
    result = lax.conv_general_dilated(
        padded_rows[None],
        flipped,
        window_strides=(1, 1, 1),
        padding=((0, 2), (0, 0), (1, 1)),
        dimension_numbers=("NDHCW", "DHWIO", "NDHCW"),
        preferred_element_type=jnp.float32,
    )
    return result[0]


def conv_weight_grad(padded_rows, grad_out):
    result = lax.conv_general_dilated(
        padded_rows[None],
        grad_out[None],
        window_strides=(1, 1, 1),
        padding=((2, 0), (0, 0), (1, 1)),
        dimension_numbers=("CDHNW", "IDHOW", "NDHCW"),
        preferred_element_type=jnp.float32,
    )
    return jnp.transpose(result, (1, 2, 4, 3, 0))


def norm_inverse(values):
    return lax.rsqrt(jnp.mean(values * values, axis=2, keepdims=True) + epsilon)


def norm_backward(grad_act, normed, inverse, norm_gain):
    gained = normed * norm_gain[None, None, :, None]
    sigmoid_unit = jax.nn.sigmoid(gained)
    scaled = (
        grad_act.astype(jnp.float32)
        * sigmoid_unit
        * (1.0 + gained * (1.0 - sigmoid_unit))
        * norm_gain[None, None, :, None]
    )
    mean_two = jnp.mean(scaled * normed, axis=2, keepdims=True)
    return inverse * (scaled - normed * mean_two)


def local(
    decoder_input,
    reward_grad,
    reward_owner,
    scored_frame,
    first_gain,
    second_gain,
    first_kernel,
    second_kernel,
):
    tile_count = lax.axis_size("tile")
    arrived, reward_rows = (
        lax.all_to_all(decoder_input, "tile", split_axis=2, concat_axis=1, tiled=True),
        lax.all_to_all(reward_grad, "tile", split_axis=2, concat_axis=1, tiled=True),
    )
    features = arrived[0]
    reward_rows = reward_rows[0]
    frames, rows_local, channels, col_count = features.shape
    grad_scale = 1.0 / math.sqrt(
        lax.axis_size("clip") * frames * rows_local * tile_count * col_count
    )
    slot_map = slot_table(
        reward_owner[0, :, 0], scored_frame[0], tile_count, reward_grad.shape[1], frames
    )
    grad_out = jnp.einsum(
        "fs,shcw->fhcw",
        slot_map.astype(jnp.bfloat16),
        reward_rows,
        preferred_element_type=jnp.float32,
    ).astype(jnp.bfloat16)
    inputs_float = features.astype(jnp.float32)
    inverse_in = norm_inverse(inputs_float)
    normed_in = inputs_float * inverse_in
    act_in = jax.nn.silu(normed_in * first_gain[None, None, :, None]).astype(jnp.bfloat16)
    act_in_rows = with_halo(act_in, (("tile", 1),), 1)
    hidden = conv_forward(act_in_rows, first_kernel).astype(jnp.bfloat16)
    hidden_float = hidden.astype(jnp.float32)
    inverse_mid = norm_inverse(hidden_float)
    normed_mid = hidden_float * inverse_mid
    act_mid = jax.nn.silu(normed_mid * second_gain[None, None, :, None]).astype(jnp.bfloat16)
    both_rows = with_halo(jnp.stack([act_mid, grad_out]), (("tile", 2),), 1)
    act_mid_rows = both_rows[0]
    grad_rows = both_rows[1]
    second_local = conv_weight_grad(act_mid_rows, grad_out) * grad_scale
    second_total = second_local
    grad_mid = conv_input_grad(grad_rows, second_kernel).astype(jnp.bfloat16)
    grad_hidden = norm_backward(grad_mid, normed_mid, inverse_mid, second_gain).astype(jnp.bfloat16)
    grad_hidden_rows = with_halo(grad_hidden, (("tile", 1),), 1)
    first_local = conv_weight_grad(act_in_rows, grad_hidden) * grad_scale
    grad_in = conv_input_grad(grad_hidden_rows, first_kernel).astype(jnp.bfloat16)
    feature_local = (
        grad_out.astype(jnp.float32) + norm_backward(grad_in, normed_in, inverse_in, first_gain)
    ).astype(jnp.bfloat16)
    feature_grad = lax.all_to_all(
        feature_local[None], "tile", split_axis=1, concat_axis=2, tiled=True
    )
    first_total, second_total = lax.psum((first_local, second_total), ("clip", "tile"))
    return (feature_grad, first_total, second_total)


def solution(mesh):
    in_specs = (
        P("clip", "tile", None, None, None),
        P("clip", "tile", None, None, None),
        P("clip", None, None),
        P("clip", None),
        P(),
        P(),
        P(),
        P(),
    )
    out_specs = (P("clip", "tile", None, None, None), P(), P())
    return jax.shard_map(local, mesh=mesh, in_specs=in_specs, out_specs=out_specs, check_vma=False)
```

profile of v0, /device:TPU:1, one launch (start us, length us, event | category | flops | bytes accessed | tf_op | source)
XLA Modules:
  0.0 552.4 jit_solution(4180531474459470173)
XLA Ops:
  7.2 10.1 %all-to-all-start.1 = ((bf16[1,1,32,96,128]{4,3,1,0,2:T(8,128)(2,1)}), bf16[1,1,32,96,128]{4,3,1,0,2:T(8,128)(2,1)S(1)}, u32[]{:S(2)}, u32[]{:S(2)}) async-start(bf16[1,1,32,96,128]{4,3,1,0,2:T(8,128)(2,1)} %bitcast.177), calls=%async_computation.1 | async-start | bytes 1572864 | tf_op jit(solution)/shard_map/all_to_all | solution.py:104
  17.3 1.5 copy.58
  18.8 21.2 %all-to-all-done.1 = bf16[1,1,32,96,128]{4,3,1,0,2:T(8,128)(2,1)S(1)} async-done(((bf16[1,1,32,96,128]{4,3,1,0,2:T(8,128)(2,1)}), bf16[1,1,32,96,128]{4,3,1,0,2:T(8,128)(2,1)S(1)}, u32[]{:S(2)}, u32[]{:S(2)}) %all-to-all-start.1) | async-done | bytes 786464 | tf_op jit(solution)/shard_map/all_to_all | solution.py:104
  40.0 4.3 all-to-all-start
  44.9 1.1 multiply_convert_fusion
  46.2 2.4 collective-permute-start
  48.7 1.9 collective-permute-start.1
  50.9 31.1 %collective-permute-done = bf16[16,1,96,128]{3,0,2,1:T(8,128)(2,1)S(1)} collective-permute-done((bf16[16,1,96,128]{3,0,2,1:T(8,128)(2,1)S(1)}, bf16[16,1,96,128]{3,0,2,1:T(8,128)(2,1)S(1)}, u32[]{:S(2)}, u32[]{:S(2)}) %collective-permute-start) | collective-permute-done | bytes 393248 | tf_op jit(solution)/shard_map/ppermute | solution.py:16
  82.0 1.7 collective-permute-done.1
  83.7 1.9 fusion.64
  85.6 4.4 copy.96
  90.0 0.4 pad.clone
  90.4 0.6 copy.66
  91.1 7.9 %select_convert_fusion.2 = bf16[16,2,8,17,96]{4,2,3,1,0:T(8,128)(2,1)S(1)} fusion(bf16[3,3,3,96,96]{4,3,2,1,0:T(8,128)(2,1)S(1)} %copy-done, bf16[16,4,96,1,7,2]{2,4,5,1,0,3:T(8,128)(2,1)S(1)} %slice.42, bf16[16,4,96,1,8,17]{2,4,5,1,0,3:T(8,128)(2,1)S(1)} %copy.66, pred[8,17]{0,1:T(8,128)(4,1)S(1)} %copy-done.31), kind=kOutput, calls=%fused_computation.25 | convolution fusion | flops 2036908032 | bytes 3176584 | tf_op jit(solution)/shard_map/conv_general_dilated | solution.py:39
  99.1 0.3 copy.67
  99.4 1.6 copy.69
  101.2 1.4 copy.91
  102.6 3.1 slice.44
  105.7 2.7 copy.92
  108.6 0.8 copy-done.17
  109.4 1.4 fusion.49
  110.8 3.9 copy.59
  114.7 2.0 convolution_convert_fusion
  116.7 1.4 fusion.62
  118.1 2.7 collective-permute-start.2
  120.8 2.5 collective-permute-start.3
  123.3 7.7 %copy.84 = bf16[1,16,4,96,128]{3,0,4,2,1:T(2,128)(2,1)} copy(bf16[1,16,4,96,128]{4,1,3,2,0:T(8,128)(2,1)} %get-tuple-element.16) | data formatting | bytes 3145728 | tf_op jit(solution)/shard_map/broadcast_in_dim | solution.py:40
  131.0 2.7 copy.87
  133.7 0.7 collective-permute-done.3
  134.4 1.6 pad_maximum_fusion
  136.0 2.2 fusion.79
  138.2 3.9 copy.97
  142.2 0.4 pad.2.clone
  142.6 0.6 copy.73
  143.3 0.4 copy-done.30
  143.7 7.0 %select_convert_fusion.1 = bf16[16,2,8,17,96]{4,2,3,1,0:T(8,128)(2,1)S(1)} fusion(bf16[3,3,3,96,96]{4,3,2,1,0:T(8,128)(2,1)S(1)} %copy-done.30, bf16[16,4,96,1,7,2]{2,4,5,1,0,3:T(8,128)(2,1)S(1)} %slice.48, bf16[16,4,96,1,8,17]{2,4,5,1,0,3:T(8,128)(2,1)S(1)} %copy.73, pred[8,17]{0,1:T(8,128)(4,1)S(1)} %copy-done.31), kind=kOutput, calls=%fused_computation.24 | convolution fusion | flops 2036908032 | bytes 3176584 | tf_op jit(solution)/shard_map/conv_general_dilated | solution.py:52
  151.0 1.6 copy.82
  152.8 1.4 copy.93
  154.2 0.9 fusion.41
  155.2 1.0 fusion.44
  156.2 1.1 fusion.80
  157.3 2.3 collective-permute-start.4
  159.6 2.7 collective-permute-start.5
  162.5 2.2 copy.95
  164.7 7.8 %copy.86 = bf16[1,16,4,96,128]{3,0,4,2,1:T(2,128)(2,1)} copy(bf16[1,16,4,96,128]{4,1,3,2,0:T(8,128)(2,1)} %get-tuple-element.14) | data formatting | bytes 3145728 | tf_op jit(solution)/shard_map/slice | solution.py:133
  172.6 34.4 %convolution_multiply_fusion = f32[3,3,3,96,96]{3,4,2,1,0:T(8,128)} fusion(bf16[1,16,4,96,128]{3,0,4,2,1:T(2,128)(2,1)} %copy.86, bf16[1,16,2,96,128]{3,0,4,2,1:T(2,128)(2,1)S(1)} %copy-done.13), kind=kOutput, calls=%fused_computation.73 | convolution fusion | flops 1901325312 | bytes 3354624 | tf_op jit(solution)/shard_map/transpose | solution.py:72
  207.0 0.9 fusion.29
  208.0 2.7 copy.85
  210.7 2.4 maximum_bitcast_fusion
  213.1 3.9 copy.98
  217.1 0.4 pad.4.clone
  217.5 0.6 copy.78
  218.2 7.0 %select_convert_fusion = bf16[16,2,8,17,96]{4,2,3,1,0:T(8,128)(2,1)S(1)} fusion(bf16[3,3,3,96,96]{4,3,2,1,0:T(8,128)(2,1)S(1)} %copy-done, bf16[16,4,96,1,7,2]{2,4,5,1,0,3:T(8,128)(2,1)S(1)} %slice.52, bf16[16,4,96,1,8,17]{2,4,5,1,0,3:T(8,128)(2,1)S(1)} %copy.78, pred[8,17]{0,1:T(8,128)(4,1)S(1)} %copy-done.32), kind=kOutput, calls=%fused_computation.23 | convolution fusion | flops 2036908032 | bytes 3176584 | tf_op jit(solution)/shard_map/conv_general_dilated | solution.py:52
  225.5 1.2 slice.53
  226.7 2.4 copy.94
  229.1 1.4 multiply_reduce_fusion
  230.5 1.5 fusion.61
  232.0 1.1 copy.81
  233.1 8.9 %all-to-all-start.2 = ((bf16[1,16,2,96,128]{4,3,2,0,1:T(8,128)(2,1)}), bf16[1,16,2,96,128]{4,3,2,0,1:T(8,128)(2,1)}, u32[]{:S(2)}, u32[]{:S(2)}) async-start(bf16[1,16,2,96,128]{4,3,2,0,1:T(8,128)(2,1)} %copy.81), calls=%async_computation.2 | async-start | bytes 1572864 | tf_op jit(solution)/shard_map/all_to_all | solution.py:145
  242.0 33.9 %convolution_multiply_fusion.1 = f32[3,3,3,96,96]{3,4,2,1,0:T(8,128)} fusion(bf16[1,16,4,96,128]{3,0,4,2,1:T(2,128)(2,1)} %copy.84, bf16[1,16,2,96,128]{3,0,4,2,1:T(2,128)(2,1)S(1)} %copy-done.14), kind=kOutput, calls=%fused_computation.74 | convolution fusion | flops 1901325312 | bytes 3354624 | tf_op jit(solution)/shard_map/transpose | solution.py:72
  275.9 262.9 %all-reduce.3.cloned.1.call-done = (f32[3,3,3,96,96]{3,4,2,1,0:T(8,128)}, f32[3,3,3,96,96]{3,4,2,1,0:T(8,128)}) async-done(((f32[3,3,3,96,96]{3,4,2,1,0:T(8,128)}, f32[3,3,3,96,96]{3,4,2,1,0:T(8,128)}), (f32[3,3,3,96,96]{3,4,2,1,0:T(8,128)}, f32[3,3,3,96,96]{3,4,2,1,0:T(8,128)})) %all-reduce.3.cloned.1.call-update) | async-done | bytes 1990672 | tf_op jit(solution)/shard_map/psum | solution.py:148
  538.9 2.9 copy.88
  541.8 1.5 copy.89
  543.3 2.1 copy.117
  (92 shorter events, 2.8 us)
Async XLA Ops:
  7.2 83.9 %copy-start = (bf16[3,3,3,96,96]{4,3,2,1,0:T(8,128)(2,1)S(1)}, bf16[3,3,3,96,96]{4,3,2,1,0:T(8,128)(2,1)}, u32[]{:S(2)}) copy-start(bf16[3,3,3,96,96]{4,3,2,1,0:T(8,128)(2,1)} %param.14) | copy-start | bytes 1492996
  7.2 10.1 %copy-start.15 = (bf16[1,2,32,96,128]{4,3,2,1,0:T(8,128)(2,1)S(1)}, bf16[1,2,32,96,128]{4,3,2,1,0:T(8,128)(2,1)}, u32[]{:S(2)}) copy-start(bf16[1,2,32,96,128]{4,3,2,1,0:T(8,128)(2,1)} %param.9) | copy-start | bytes 4718596
  7.2 32.8 %all-to-all-start.1 = ((bf16[1,1,32,96,128]{4,3,1,0,2:T(8,128)(2,1)}), bf16[1,1,32,96,128]{4,3,1,0,2:T(8,128)(2,1)S(1)}, u32[]{:S(2)}, u32[]{:S(2)}) async-start(bf16[1,1,32,96,128]{4,3,1,0,2:T(8,128)(2,1)} %bitcast.177), calls=%async_computation.1 | async-start | bytes 1572864 | tf_op jit(solution)/shard_map/all_to_all | solution.py:104
  40.0 70.8 %all-to-all-start = ((bf16[1,2,32,96,128]{4,3,1,0,2:T(8,128)(2,1)}), bf16[1,2,32,96,128]{4,3,1,0,2:T(8,128)(2,1)}, u32[]{:S(2)}, u32[]{:S(2)}) async-start(bf16[1,2,32,96,128]{4,3,1,0,2:T(8,128)(2,1)} %copy.58), calls=%async_computation | async-start | bytes 3145728 | tf_op jit(solution)/shard_map/all_to_all | solution.py:105
  44.3 0.7 copy-start.26
  44.7 1.6 copy-start.2
  44.7 1.5 copy-start.20
  44.9 5.7 %copy-start.28 = (s32[1,16,1]{1,2,0:T(1,128)S(1)}, s32[1,16,1]{1,2,0:T(1,128)}, u32[]{:S(2)}) copy-start(s32[1,16,1]{1,2,0:T(1,128)} %param.10) | copy-start | bytes 196
  46.2 35.8 %collective-permute-start = (bf16[16,1,96,128]{3,0,2,1:T(8,128)(2,1)S(1)}, bf16[16,1,96,128]{3,0,2,1:T(8,128)(2,1)S(1)}, u32[]{:S(2)}, u32[]{:S(2)}) collective-permute-start(bf16[16,1,96,128]{3,0,2,1:T(8,128)(2,1)S(1)} %get-tuple-element.22), channel_id=1, source_target_pairs={{0,1},{1,2},{2,3},{3,4},{4,5},{5,6},{6,7},{7,8},{8,9},{9,10},{10,1... | collective-permute-start | bytes 1179656 | tf_op jit(solution)/shard_map/ppermute | solution.py:16
  48.7 35.0 %collective-permute-start.1 = (bf16[16,1,96,128]{3,0,2,1:T(8,128)(2,1)S(1)}, bf16[16,1,96,128]{3,0,2,1:T(8,128)(2,1)S(1)}, u32[]{:S(2)}, u32[]{:S(2)}) collective-permute-start(bf16[16,1,96,128]{3,0,2,1:T(8,128)(2,1)S(1)} %get-tuple-element.23), channel_id=1, source_target_pairs={{1,0},{2,1},{3,2},{4,3},{5,4},{6,5},{7,6},{8,7},{9,8},{10,9},{11,1... | collective-permute-start | bytes 1179656 | tf_op jit(solution)/shard_map/ppermute | solution.py:19
  90.4 0.7 copy-start.31
  105.7 3.7 copy-start.24
  108.4 2.4 copy-start.6
  108.6 0.8 copy-start.17
  110.8 3.9 copy-start.29
  114.7 2.0 copy-start.9
  116.7 17.7 %copy-start.4 = (bf16[16,2,96,128]{3,0,2,1:T(8,128)(2,1)}, bf16[16,2,96,128]{3,0,2,1:T(8,128)(2,1)S(1)}, u32[]{:S(2)}) copy-start(bf16[16,2,96,128]{3,0,2,1:T(8,128)(2,1)S(1)} %convolution_convert_fusion) | copy-start | bytes 2359300
  118.1 15.6 %collective-permute-start.2 = (bf16[2,16,1,96,128]{4,1,3,2,0:T(8,128)(2,1)}, bf16[2,16,1,96,128]{4,1,3,2,0:T(8,128)(2,1)}, u32[]{:S(2)}, u32[]{:S(2)}) collective-permute-start(bf16[2,16,1,96,128]{4,1,3,2,0:T(8,128)(2,1)} %get-tuple-element.18), channel_id=1, source_target_pairs={{0,1},{1,2},{2,3},{3,4},{4,5},{5,6},{6,7},{7,8},{8,9},{9,10},{10,1... | collective-permute-start | bytes 2359304 | tf_op jit(solution)/shard_map/ppermute | solution.py:16
  120.8 13.6 %collective-permute-start.3 = (bf16[2,16,1,96,128]{4,1,3,2,0:T(8,128)(2,1)}, bf16[2,16,1,96,128]{4,1,3,2,0:T(8,128)(2,1)}, u32[]{:S(2)}, u32[]{:S(2)}) collective-permute-start(bf16[2,16,1,96,128]{4,1,3,2,0:T(8,128)(2,1)} %get-tuple-element.19), channel_id=1, source_target_pairs={{1,0},{2,1},{3,2},{4,3},{5,4},{6,5},{7,6},{8,7},{9,8},{10,9},{11,1... | collective-permute-start | bytes 2359304 | tf_op jit(solution)/shard_map/ppermute | solution.py:19
  142.6 1.1 copy-start.30
  152.6 1.6 copy-start.18
  155.1 2.1 copy-start.22
  155.1 7.2 %copy-start.8 = (f32[16,2,8,17,96]{4,0,3,2,1:T(8,128)S(1)}, f32[16,2,8,17,96]{4,0,3,2,1:T(8,128)}, u32[]{:S(2)}) copy-start(f32[16,2,8,17,96]{4,0,3,2,1:T(8,128)} %copy.82) | copy-start | bytes 5013508
  156.2 6.2 %copy-start.10 = (bf16[16,2,96,128]{3,0,2,1:T(8,128)(2,1)}, bf16[16,2,96,128]{3,0,2,1:T(8,128)(2,1)S(1)}, u32[]{:S(2)}) copy-start(bf16[16,2,96,128]{3,0,2,1:T(8,128)(2,1)S(1)} %fusion.44) | copy-start | bytes 2359300
  157.3 53.4 %collective-permute-start.4 = (bf16[16,1,96,128]{3,0,2,1:T(8,128)(2,1)}, bf16[16,1,96,128]{3,0,2,1:T(8,128)(2,1)}, u32[]{:S(2)}, u32[]{:S(2)}) collective-permute-start(bf16[16,1,96,128]{3,0,2,1:T(8,128)(2,1)} %get-tuple-element.20), channel_id=1, source_target_pairs={{0,1},{1,2},{2,3},{3,4},{4,5},{5,6},{6,7},{7,8},{8,9},{9,10},{10,1... | collective-permute-start | bytes 1179656 | tf_op jit(solution)/shard_map/ppermute | solution.py:16
  159.6 51.0 %collective-permute-start.5 = (bf16[16,1,96,128]{3,0,2,1:T(8,128)(2,1)}, bf16[16,1,96,128]{3,0,2,1:T(8,128)(2,1)}, u32[]{:S(2)}, u32[]{:S(2)}) collective-permute-start(bf16[16,1,96,128]{3,0,2,1:T(8,128)(2,1)} %get-tuple-element.21), channel_id=1, source_target_pairs={{1,0},{2,1},{3,2},{4,3},{5,4},{6,5},{7,6},{8,7},{9,8},{10,9},{11,1... | collective-permute-start | bytes 1179656 | tf_op jit(solution)/shard_map/ppermute | solution.py:19
  164.7 7.8 %copy-start.13 = (bf16[1,16,2,96,128]{3,0,4,2,1:T(2,128)(2,1)S(1)}, bf16[1,16,2,96,128]{3,0,4,2,1:T(2,128)(2,1)}, u32[]{:S(2)}) copy-start(bf16[1,16,2,96,128]{3,0,4,2,1:T(2,128)(2,1)} %copy.87) | copy-start | bytes 2359300
  172.5 34.5 %copy-start.7 = (f32[16,2,1,128,96]{3,0,4,1,2:T(8,128)S(1)}, f32[16,2,1,128,96]{3,0,4,1,2:T(8,128)}, u32[]{:S(2)}) copy-start(f32[16,2,1,128,96]{3,0,4,1,2:T(8,128)} %copy-done.6) | copy-start | bytes 4718596
  172.5 34.5 %copy-start.12 = (f32[16,2,1,128,96]{3,0,4,1,2:T(8,128)S(1)}, f32[16,2,1,128,96]{3,0,4,1,2:T(8,128)}, u32[]{:S(2)}) copy-start(f32[16,2,1,128,96]{3,0,4,1,2:T(8,128)} %copy.95) | copy-start | bytes 4718596
  172.5 34.5 %copy-start.19 = (f32[16,2,128]{2,0,1:T(8,128)S(1)}, f32[16,2,128]{2,0,1:T(8,128)}, u32[]{:S(2)}) copy-start(f32[16,2,128]{2,0,1:T(8,128)} %copy-done.17) | copy-start | bytes 49156
  172.5 34.5 %copy-start.23 = (f32[16,2,128]{2,0,1:T(8,128)S(1)}, f32[16,2,128]{2,0,1:T(8,128)}, u32[]{:S(2)}) copy-start(f32[16,2,128]{2,0,1:T(8,128)} %copy-done.22) | copy-start | bytes 49156
  172.6 34.5 %copy-start.25 = (f32[96]{0:T(128)S(1)}, f32[96]{0:T(128)}, u32[]{:S(2)}) copy-start(f32[96]{0:T(128)} %param.13) | copy-start | bytes 1156
  208.0 2.7 copy-start.11
  217.5 0.7 copy-start.32
  225.5 3.6 copy-start.3
  225.5 3.6 copy-start.21
  225.5 3.6 copy-start.27
  229.1 1.4 copy-start.5
  232.0 10.1 %copy-start.14 = (bf16[1,16,2,96,128]{3,0,4,2,1:T(2,128)(2,1)S(1)}, bf16[1,16,2,96,128]{3,0,4,2,1:T(2,128)(2,1)}, u32[]{:S(2)}) copy-start(bf16[1,16,2,96,128]{3,0,4,2,1:T(2,128)(2,1)} %copy.85) | copy-start | bytes 2359300
  233.1 310.2 %all-to-all-start.2 = ((bf16[1,16,2,96,128]{4,3,2,0,1:T(8,128)(2,1)}), bf16[1,16,2,96,128]{4,3,2,0,1:T(8,128)(2,1)}, u32[]{:S(2)}, u32[]{:S(2)}) async-start(bf16[1,16,2,96,128]{4,3,2,0,1:T(8,128)(2,1)} %copy.81), calls=%async_computation.2 | async-start | bytes 1572864 | tf_op jit(solution)/shard_map/all_to_all | solution.py:145
  242.0 296.9 %all-reduce.3.cloned.1.call-start = ((), (), s32[]{:S(2)}) async-start(), calls=%async_computation.3 | async-start | bytes 5308416 | tf_op jit(solution)/shard_map/psum | solution.py:148
  538.9 2.9 copy-start.16
  541.8 3.6 copy-start.1
Sparse Core Ops, SparseCore 0:
  276.0 262.7 all-reduce.2
where the time goes:
time: 558 us; the launch traced here: 552 us
  waiting for transfers between devices  318 us (57%)
  matrix products  92.2 us (17%)
  local copies, waits for them, and re-layouts  73.3 us (13%)
  starting transfers between devices  38 us (7%)
  other arithmetic  16.3 us (3%)
  between operations  15 us (3%)
    psum x1, waiting for transfers between devices, local(): lax.psum((first_local, second_total), ('clip', 'tile'))  263 us
    transpose x2, matrix products, conv_weight_grad(): return jnp.transpose(result, (1, 2, 4, 3, 0))  68.3 us
    unnamed x78, local copies, waits for them, and re-layouts  31.9 us
    ppermute x3, waiting for transfers between devices, with_halo(): lax.ppermute(lax.slice_in_dim(block, block.shape[dim] - width, None, axis...  31.1 us
    all_to_all x1, waiting for transfers between devices, local(): lax.all_to_all(decoder_input, 'tile', split_axis=2, concat_axis=1, tiled=...  21.2 us
    conv_general_dilated x2, matrix products, conv_input_grad(): lax.conv_general_dilated(padded_rows[None], flipped, window_strides=(1, 1...  14 us
  transfers between devices with their start and end apart: 10, of which 5 were waited for; matrix products, arithmetic and copies ran while one was open for 23% of the time, Pallas kernels for 0%

commit v1 on v0

v1 whole, which is shorter than its diff:
```python
import functools

import jax
import jax.numpy as jnp
from jax import lax
from jax.experimental import pallas as pl
from jax.experimental.pallas import tpu as pltpu
from jax.sharding import PartitionSpec as P

MESH = pl.DeviceIdType.MESH
F32 = jnp.float32
BF16 = jnp.bfloat16
epsilon = 1e-06

FRAMES = 16
TILES = 16
CLIPS = 16
C = 96
W = 128
TAPS = 9 * C
PADDED = 896
UNROLL = 2


def inverse_rms(x):
    return lax.rsqrt(jnp.mean(x * x, axis=0, keepdims=True) + epsilon)


def sigmoid(u):
    return 0.5 * jnp.tanh(0.5 * u) + 0.5


def norm_silu(x, gain):
    u = gain * (x * inverse_rms(x))
    return u * sigmoid(u)


def norm_backward(g, x, gain):
    r = inverse_rms(x)
    normed = x * r
    u = gain * normed
    sig = sigmoid(u)
    q = g * gain * sig * (1.0 + u * (1.0 - sig))
    p = jnp.mean(q * normed, axis=0, keepdims=True)
    return r * (q - normed * p)


def put_row(y_ref, f, r, value):
    lane = lax.broadcasted_iota(jnp.int32, (C, W), 1)
    wide = value.astype(F32)
    low = jnp.where(lane == 0, 0.0, pltpu.roll(wide, 1, 1)).astype(BF16)
    high = jnp.where(lane == W - 1, 0.0, pltpu.roll(wide, W - 1, 1)).astype(BF16)
    for e, v in enumerate((low, value, high)):
        for b in range(3):
            h = r - b
            if 0 <= h < 2:
                y_ref[f, (b * 3 + e) * C:(b * 3 + e + 1) * C, h * W:(h + 1) * W] = v


def kernel(
    x_ref, rw_ref, own_col_ref, own_row_ref, scored_ref, g1_ref, g2_ref, k1_ref, k2_ref,
    out_ref, res_ref,
    rin, rrw, k1f, k1t, k2t, g1c, g2c, pick,
    x4, xg4, xh4, yin, yg, yh, hid, act, gh, c1, c2, fb,
    w1, w2, bb, r0, r1, cc, r2,
    in_s, in_r, rw_s, rw_r, loc, halo_s, halo_r, f_s, f_r,
    s0_s, s0_r, s1_s, s1_r, s2_s, s2_r, a2_s, a2_r, a1_s, a1_r, a0_s, a0_r,
):
    clip = lax.axis_index("clip")
    me = lax.axis_index("tile")
    core = me % 2
    z = me // 2
    sibling = me + 1 - 2 * core

    def tile_peer(i):
        step = i // 2 + 1
        return (me + (1 - i % 2) * step + (i % 2) * (TILES - step)) % TILES

    def clip_peer(i):
        return (clip + i + 1) % CLIPS

    def z_peer(i):
        return ((z + i + 1) % 8) * 2 + core

    def loop(n, body):
        def step(i, carry):
            body(i)
            return carry

        lax.fori_loop(0, n, step, 0)

    barrier = pltpu.get_barrier_semaphore()
    loop(15, lambda i: pl.semaphore_signal(
        barrier, inc=1, device_id=(clip, tile_peer(i)), device_id_type=MESH))
    loop(15, lambda i: pl.semaphore_signal(
        barrier, inc=1, device_id=(clip_peer(i), me), device_id_type=MESH))
    pl.semaphore_wait(barrier, 30)

    def in_copy(src, dst, slot, peer):
        return pltpu.make_async_remote_copy(
            src_ref=x_ref.at[pl.ds(2 * src, 2)], dst_ref=rin.at[dst],
            send_sem=in_s.at[src], recv_sem=in_r.at[slot],
            device_id=(clip, peer), device_id_type=MESH)

    def rw_copy(src, dst, slot, peer):
        return pltpu.make_async_remote_copy(
            src_ref=rw_ref.at[:, pl.ds(2 * src, 2)], dst_ref=rrw.at[dst],
            send_sem=rw_s.at[src], recv_sem=rw_r.at[slot],
            device_id=(clip, peer), device_id_type=MESH)

    own_in = pltpu.make_async_copy(x_ref.at[pl.ds(2 * me, 2)], rin.at[me], loc.at[0])
    own_rw = pltpu.make_async_copy(rw_ref.at[:, pl.ds(2 * me, 2)], rrw.at[me], loc.at[1])

    def start_in(i):
        peer = tile_peer(14 - i)
        in_copy(peer, me, me, peer).start()

    def start_rw(i):
        peer = tile_peer(14 - i)
        rw_copy(peer, me, me, peer).start()

    loop(15, start_in)
    own_in.start()
    loop(15, start_rw)
    own_rw.start()

    def column(row_ref):
        row = lax.broadcasted_iota(jnp.int32, (C, C), 0)
        col = lax.broadcasted_iota(jnp.int32, (C, C), 1)
        wide = jnp.broadcast_to(row_ref[...], (C, C))
        return jnp.broadcast_to(
            jnp.sum(jnp.where(row == col, wide, 0.0), axis=1, keepdims=True), (C, W))

    g1c[...] = column(g1_ref)
    g2c[...] = column(g2_ref)

    own_col, own_row = own_col_ref[...], own_row_ref[...]
    earlier = (lax.broadcasted_iota(jnp.int32, (16, 16), 1)
               < lax.broadcasted_iota(jnp.int32, (16, 16), 0))
    same = own_col == own_row
    ranking = jnp.sum(jnp.where(same & earlier, 1, 0), axis=1, keepdims=True)
    slot = own_col * 2 + ranking
    by_slot = jnp.where(
        slot == lax.shift_right_logical(lax.broadcasted_iota(jnp.int32, (16, 512), 1), 4),
        1.0, 0.0)
    by_frame = jnp.where(
        scored_ref[...]
        == lax.shift_right_logical(lax.broadcasted_iota(jnp.int32, (256, 16), 0), 4),
        1.0, 0.0)
    table = jnp.dot(by_frame, by_slot, preferred_element_type=F32)
    row16 = lax.broadcasted_iota(jnp.int32, (256, 512), 0) & 15
    col16 = lax.broadcasted_iota(jnp.int32, (256, 512), 1) & 15
    pick[...] = jnp.where(row16 == col16, table, 0.0).astype(BF16)

    for a in range(3):
        rows = slice(a * C, (a + 1) * C)
        k1f[rows, :] = jnp.concatenate(
            [k1_ref[a * 9 + i].astype(F32) for i in range(9)], axis=1).astype(BF16)
        k1t[rows, :] = jnp.transpose(jnp.concatenate(
            [k1_ref[a * 9 + 8 - i] for i in range(9)], axis=0).astype(F32)).astype(BF16)
        k2t[rows, :] = jnp.transpose(jnp.concatenate(
            [k2_ref[a * 9 + 8 - i] for i in range(9)], axis=0).astype(F32)).astype(BF16)

    act[0:2] = jnp.zeros((2, C, 2 * W), BF16)
    gh[16:18] = jnp.zeros((2, C, 2 * W), BF16)
    w1[...] = jnp.zeros_like(w1)
    w2[...] = jnp.zeros_like(w2)
    bb[252:256] = jnp.zeros((4, 2, 8, 128), F32)

    low_peer, high_peer = (me + TILES - 1) % TILES, (me + 1) % TILES

    def halo_pair(ref, k):
        up = pltpu.make_async_remote_copy(
            src_ref=ref.at[2], dst_ref=ref.at[0],
            send_sem=halo_s.at[2 * k], recv_sem=halo_r.at[2 * k],
            device_id=(clip, high_peer), device_id_type=MESH)
        down = pltpu.make_async_remote_copy(
            src_ref=ref.at[1], dst_ref=ref.at[3],
            send_sem=halo_s.at[2 * k + 1], recv_sem=halo_r.at[2 * k + 1],
            device_id=(clip, low_peer), device_id_type=MESH)
        return up, down

    def put_halo(ref, y_ref):
        def body(f):
            put_row(y_ref, f, 0, jnp.where(me > 0, ref[0, f].astype(F32), 0.0).astype(BF16))
            put_row(y_ref, f, 3, jnp.where(me < TILES - 1, ref[3, f].astype(F32), 0.0).astype(BF16))

        loop(FRAMES, body)

    def first(f):
        for h in range(2):
            v = norm_silu(rin[f, h].astype(F32), g1c[...]).astype(BF16)
            x4[1 + h, f] = v
            put_row(yin, f, 1 + h, v)

    own_in.wait()
    first(me)

    def arrived(i):
        src = tile_peer(i)
        in_copy(src, src, src, src).wait_recv()
        first(src)

    loop(15, arrived)
    halo = halo_pair(x4, 0)
    for copy in halo:
        copy.start()
    for copy in halo:
        copy.wait()
    put_halo(x4, yin)

    def conv(kernel_ref, y_ref, reverse, each):
        c1[...] = jnp.zeros_like(c1)
        c2[...] = jnp.zeros_like(c2)

        def body(i):
            one, two = c1[...], c2[...]
            for k in range(UNROLL):
                f = i * UNROLL + k
                if reverse:
                    f = FRAMES - 1 - f
                p = jnp.dot(kernel_ref[...], y_ref[f], preferred_element_type=F32)
                each(f, (p[2 * C:] + one).astype(BF16))
                one = p[C:2 * C] + two
                two = p[:C]
            c1[...] = one
            c2[...] = two

        loop(FRAMES // UNROLL, body)

    def mid(f, h):
        hid[f] = h
        for row in range(2):
            lanes = slice(row * W, (row + 1) * W)
            act[f + 2, :, lanes] = norm_silu(h[:, lanes].astype(F32), g2c[...]).astype(BF16)

    conv(k1f, yin, False, mid)

    def rw_arrived(i):
        src = tile_peer(i)
        rw_copy(src, src, src, src).wait_recv()

    own_rw.wait()
    loop(15, rw_arrived)
    for i in range(C // 16):
        rows = slice(16 * i, 16 * i + 16)
        slots = jnp.concatenate(
            [rrw[:, :, h, rows, :].reshape(512, W) for h in range(2)], axis=1)
        og = jnp.dot(pick[...], slots, preferred_element_type=F32).astype(BF16)
        og = og.reshape(FRAMES, 16, 2 * W)
        xg4[1, :, rows, :] = og[:, :, :W]
        xg4[2, :, rows, :] = og[:, :, W:]
    halo = halo_pair(xg4, 1)
    for copy in halo:
        copy.start()

    def put_own(ref, y_ref):
        def body(f):
            for h in range(2):
                put_row(y_ref, f, 1 + h, ref[1 + h, f])

        loop(FRAMES, body)

    put_own(xg4, yg)
    for copy in halo:
        copy.wait()
    put_halo(xg4, yg)

    def back_mid(f, g):
        for row in range(2):
            lanes = slice(row * W, (row + 1) * W)
            v = norm_backward(
                g[:, lanes].astype(F32), hid[f, :, lanes].astype(F32), g2c[...]).astype(BF16)
            xh4[1 + row, f] = v
            gh[f, :, lanes] = v
            put_row(yh, f, 1 + row, v)

    conv(k2t, yg, True, back_mid)
    halo = halo_pair(xh4, 2)
    for copy in halo:
        copy.start()

    def weight(left, y_ref, w_ref):
        def body(i):
            total = w_ref[:, :TAPS]
            for k in range(4):
                f = i * 4 + k
                total = total + lax.dot_general(
                    left(f), y_ref[f], (((1,), (1,)), ((), ())), preferred_element_type=F32)
            w_ref[:, :TAPS] = total

        loop(FRAMES // 4, body)

    weight(lambda f: jnp.concatenate([gh[f + 2], gh[f + 1], gh[f]], axis=0), yin, w1)
    weight(lambda f: act[pl.ds(f, 3)].reshape(3 * C, 2 * W), yg, w2)

    def pack(i):
        for n, w_ref in enumerate((w1, w2)):
            rows = w_ref[pl.ds(pl.multiple_of(8 * i, 8), 8), :]
            for j in range(7):
                bb[7 * i + j, n] = rows[:, 128 * j:128 * (j + 1)]

    loop(36, pack)
    mine, other = core * 128, (1 - core) * 128
    s0 = pltpu.make_async_remote_copy(
        src_ref=bb.at[pl.ds(other, 128)], dst_ref=r0, send_sem=s0_s.at[0], recv_sem=s0_r.at[0],
        device_id=(clip, sibling), device_id_type=MESH)
    s0.start()

    for copy in halo:
        copy.wait()
    put_halo(xh4, yh)

    s0.wait()

    def add0(i):
        at = pl.ds(mine + 8 * i, 8)
        bb[at] = bb[at] + r0[pl.ds(8 * i, 8)]

    loop(16, add0)

    def s1_copy(piece, slot_at, peer):
        return pltpu.make_async_remote_copy(
            src_ref=bb.at[pl.ds(mine + 8 * piece, 8)], dst_ref=r1.at[slot_at],
            send_sem=s1_s.at[piece], recv_sem=s1_r.at[slot_at],
            device_id=(peer, me), device_id_type=MESH)

    loop(15, lambda i: s1_copy(clip_peer(i), clip, clip_peer(i)).start())

    def f_copy(f, dst_rows, slot_at, peer):
        return pltpu.make_async_remote_copy(
            src_ref=fb.at[f], dst_ref=out_ref.at[pl.ds(2 * dst_rows, 2)],
            send_sem=f_s.at[f], recv_sem=f_r.at[slot_at],
            device_id=(clip, peer), device_id_type=MESH)

    own_out = pltpu.make_async_copy(fb.at[me], out_ref.at[pl.ds(2 * me, 2)], loc.at[2])

    def back_in(f, g):
        for row in range(2):
            v = norm_backward(
                g[:, row * W:(row + 1) * W].astype(F32), rin[f, row].astype(F32), g1c[...])
            fb[f, row] = (xg4[1 + row, f].astype(F32) + v).astype(BF16)

        @pl.when(f != me)
        def _():
            f_copy(f, me, me, f).start()

        @pl.when(f == me)
        def _():
            own_out.start()

    conv(k1t, yh, True, back_in)

    loop(15, lambda i: s1_copy(clip_peer(i), clip_peer(i), clip_peer(i)).wait())
    r1[clip] = bb[pl.ds(mine + 8 * clip, 8)]

    def add1(i):
        total = r1[0, i]
        for p in range(1, CLIPS):
            total = total + r1[p, i]
        cc[i] = total

    loop(8, add1)

    def s2_copy(zz, slot_at, peer):
        return pltpu.make_async_remote_copy(
            src_ref=cc.at[zz], dst_ref=r2.at[slot_at],
            send_sem=s2_s.at[zz], recv_sem=s2_r.at[slot_at],
            device_id=(clip, peer), device_id_type=MESH)

    def z_of(i):
        return (z + i + 1) % 8

    loop(7, lambda i: s2_copy(z_of(i), z, z_peer(i)).start())
    r2[z] = cc[z]
    loop(7, lambda i: s2_copy(z_of(i), z_of(i), z_peer(i)).wait())
    total = r2[0]
    for p in range(1, 8):
        total = total + r2[p]
    base = mine + 8 * clip
    res_ref[base + z] = total

    def a2_copy(at, sem_at, peer):
        return pltpu.make_async_remote_copy(
            src_ref=res_ref.at[base + at], dst_ref=res_ref.at[base + at],
            send_sem=a2_s.at[sem_at], recv_sem=a2_r.at[at],
            device_id=(clip, peer), device_id_type=MESH)

    loop(7, lambda i: a2_copy(z, z_of(i), z_peer(i)).start())

    def a2_wait(i):
        a2_copy(z_of(i), z_of(i), z_peer(i)).wait_recv()
        a2_copy(z, z_of(i), z_peer(i)).wait_send()

    loop(7, a2_wait)

    def a1_copy(at, sem_at, peer):
        piece = res_ref.at[pl.ds(mine + 8 * at, 8)]
        return pltpu.make_async_remote_copy(
            src_ref=piece, dst_ref=piece, send_sem=a1_s.at[sem_at], recv_sem=a1_r.at[at],
            device_id=(peer, me), device_id_type=MESH)

    loop(15, lambda i: a1_copy(clip, clip_peer(i), clip_peer(i)).start())

    def a1_wait(i):
        a1_copy(clip_peer(i), clip_peer(i), clip_peer(i)).wait_recv()
        a1_copy(clip, clip_peer(i), clip_peer(i)).wait_send()

    loop(15, a1_wait)

    def a0_copy(half):
        piece = res_ref.at[pl.ds(half, 128)]
        return pltpu.make_async_remote_copy(
            src_ref=piece, dst_ref=piece, send_sem=a0_s.at[0], recv_sem=a0_r.at[0],
            device_id=(clip, sibling), device_id_type=MESH)

    a0_copy(mine).start()
    a0_copy(other).wait_recv()
    a0_copy(mine).wait_send()

    own_out.wait()

    def drain(i):
        peer = tile_peer(i)
        f_copy(peer, peer, peer, peer).wait_recv()
        f_copy(peer, me, me, peer).wait_send()
        in_copy(peer, me, me, peer).wait_send()
        rw_copy(peer, me, me, peer).wait_send()

    loop(15, drain)


def unpack(scale, p_ref, o1_ref, o2_ref, s_ref):
    for n, o_ref in enumerate((o1_ref, o2_ref)):
        def body(i, carry):
            for j in range(7):
                s_ref[pl.ds(pl.multiple_of(8 * i, 8), 8), 128 * j:128 * (j + 1)] = (
                    p_ref[7 * i + j, n] * scale)
            return carry

        lax.fori_loop(0, 36, body, 0)
        for a in range(3):
            for i in range(9):
                block = s_ref[a * C:(a + 1) * C, i * C:(i + 1) * C]
                if n == 0:
                    o_ref[a * 9 + i] = block
                else:
                    o_ref[a * 9 + 8 - i] = jnp.transpose(block)


def local(
    decoder_input, reward_grad, reward_owner, scored_frame,
    first_gain, second_gain, first_kernel, second_kernel,
):
    vmem = pl.BlockSpec(memory_space=pltpu.VMEM)
    hbm = pl.BlockSpec(memory_space=pl.ANY)
    dma = pltpu.SemaphoreType.DMA
    feature, packed = pl.pallas_call(
        kernel,
        out_shape=(
            jax.ShapeDtypeStruct((32, C, W), BF16),
            jax.ShapeDtypeStruct((256, 2, 8, 128), F32),
        ),
        in_specs=[hbm, hbm] + [vmem] * 7,
        out_specs=(hbm, vmem),
        scratch_shapes=[
            pltpu.VMEM((16, 2, C, W), BF16),
            pltpu.VMEM((16, 2, 2, C, W), BF16),
            pltpu.VMEM((3 * C, TAPS), BF16),
            pltpu.VMEM((3 * C, TAPS), BF16),
            pltpu.VMEM((3 * C, TAPS), BF16),
            pltpu.VMEM((C, W), F32),
            pltpu.VMEM((C, W), F32),
            pltpu.VMEM((256, 512), BF16),
            pltpu.VMEM((4, 16, C, W), BF16),
            pltpu.VMEM((4, 16, C, W), BF16),
            pltpu.VMEM((4, 16, C, W), BF16),
            pltpu.VMEM((16, TAPS, 2 * W), BF16),
            pltpu.VMEM((16, TAPS, 2 * W), BF16),
            pltpu.VMEM((16, TAPS, 2 * W), BF16),
            pltpu.VMEM((16, C, 2 * W), BF16),
            pltpu.VMEM((18, C, 2 * W), BF16),
            pltpu.VMEM((18, C, 2 * W), BF16),
            pltpu.VMEM((C, 2 * W), F32),
            pltpu.VMEM((C, 2 * W), F32),
            pltpu.VMEM((16, 2, C, W), BF16),
            pltpu.VMEM((3 * C, PADDED), F32),
            pltpu.VMEM((3 * C, PADDED), F32),
            pltpu.VMEM((256, 2, 8, 128), F32),
            pltpu.VMEM((128, 2, 8, 128), F32),
            pltpu.VMEM((16, 8, 2, 8, 128), F32),
            pltpu.VMEM((8, 2, 8, 128), F32),
            pltpu.VMEM((8, 2, 8, 128), F32),
            dma((16,)), dma((16,)), dma((16,)), dma((16,)), dma((3,)),
            dma((6,)), dma((6,)), dma((16,)), dma((16,)),
            dma((1,)), dma((1,)), dma((16,)), dma((16,)), dma((8,)), dma((8,)),
            dma((8,)), dma((8,)), dma((16,)), dma((16,)), dma((1,)), dma((1,)),
        ],
        compiler_params=pltpu.CompilerParams(
            collective_id=0, has_side_effects=True, vmem_limit_bytes=56 * 2**20),
    )(
        decoder_input[0, 0],
        reward_grad[0],
        reward_owner[0],
        reward_owner[0].reshape(1, 16),
        scored_frame,
        first_gain.reshape(1, C),
        second_gain.reshape(1, C),
        first_kernel.reshape(27, C, C),
        second_kernel.reshape(27, C, C),
    )
    first_total, second_total = pl.pallas_call(
        functools.partial(unpack, 1.0 / 1024.0),
        out_shape=(jax.ShapeDtypeStruct((27, C, C), F32),) * 2,
        in_specs=[vmem],
        out_specs=(vmem, vmem),
        scratch_shapes=[pltpu.VMEM((3 * C, PADDED), F32)],
        compiler_params=pltpu.CompilerParams(vmem_limit_bytes=32 * 2**20),
    )(packed)
    shape = (3, 3, 3, C, C)
    return feature[None, None], first_total.reshape(shape), second_total.reshape(shape)


def solution(mesh):
    in_specs = (
        P("clip", "tile", None, None, None),
        P("clip", "tile", None, None, None),
        P("clip", None, None),
        P("clip", None),
        P(),
        P(),
        P(),
        P(),
    )
    out_specs = (P("clip", "tile", None, None, None), P(), P())
    return jax.shard_map(local, mesh=mesh, in_specs=in_specs, out_specs=out_specs, check_vma=False)
```

time: 558 us -> 155 us (0.28)
  waiting for transfers between devices: 318 us -> 0 us
  Pallas kernels: 0 us -> 150 us
  matrix products: 92.2 us -> 0 us
  local copies, waits for them, and re-layouts: 73.3 us -> 3.8 us
  starting transfers between devices: 38 us -> 0 us
  other arithmetic: 16.3 us -> 0 us
  between operations: 15 us -> 0.65 us
    psum x1 -> x0, waiting for transfers between devices: 263 us -> none  [local(): lax.psum((first_local, second_total), ('clip', 'tile'))]
    pallas_call x0 -> x2, Pallas kernels: none -> 150 us  [the longest x1 147 us: local(): pl.pallas_call(kernel, out_shape=(jax.ShapeDtypeStruct((32, C, W), BF16),...]
    transpose x2 -> x0, matrix products: 68.3 us -> none  [conv_weight_grad(): return jnp.transpose(result, (1, 2, 4, 3, 0))]
    ppermute x6 -> x0, waiting for transfers between devices: 33.5 us -> none  [the longest x3 31.1 us: with_halo(): lax.ppermute(lax.slice_in_dim(block, block.shape[dim] - width, None, axis...]
    unnamed x78 -> x5, local copies, waits for them, and re-layouts: 31.9 us -> 2.47 us
    all_to_all x3 -> x0, starting transfers between devices: 23.3 us -> none  [the longest x1 10.1 us: local(): lax.all_to_all(decoder_input, 'tile', split_axis=2, concat_axis=1, tiled=...]
    conv_general_dilated x3 -> x0, matrix products: 21.9 us -> none  [the longest x2 14 us: conv_input_grad(): lax.conv_general_dilated(padded_rows[None], flipped, window_strides=(1, 1...]
    all_to_all x3 -> x0, waiting for transfers between devices: 21.2 us -> none  [the longest x1 21.2 us: local(): lax.all_to_all(decoder_input, 'tile', split_axis=2, concat_axis=1, tiled=...]
  transfers between devices with their start and end apart: 10 -> 0, of which waited for: 5 -> 0; matrix products, arithmetic and copies ran while one was open for 23% -> 0% of each run, Pallas kernels for 0% -> 0%
where the time goes in v1:
time: 155 us
  Pallas kernels  150 us (97%)
  local copies, waits for them, and re-layouts  3.8 us (2%)
    pallas_call x1, Pallas kernels, local(): pl.pallas_call(kernel, out_shape=(jax.ShapeDtypeStruct((32, C, W), BF16),...  147 us

profile of v1, /device:TPU:1, one launch (start us, length us, event | category | flops | bytes accessed | tf_op | source)
XLA Modules:
  0.0 154.7 jit_solution(6906345408475561814)
XLA Ops:
  0.6 1.3 copy.11.own_col_ref
  2.0 147.4 %shard_map.103 = (bf16[32,96,128]{2,1,0:T(8,128)(2,1)}, f32[256,2,8,128]{3,2,1,0:T(8,128)}) custom-call(bf16[32,96,128]{2,1,0:T(8,128)(2,1)} %bitcast.13, bf16[2,32,96,128]{3,2,1,0:T(8,128)(2,1)} %bitcast.11, s32[16,1]{1,0:T(8,128)} %copy.11.own_col_ref, s32[1,16]{1,0:T(1,128)} %bitcast.17, s32[1,16]{1,0:T(1,128)} %scored_ref.1, f32[1,96]{1,0:T(1,128)} %bitcast.18, ...), custom_call_target="tpu_custom_call" | custom-call | tf_op jit(solution)/shard_map/pallas_call | solution.py:458
  149.4 0.0 copy-start
  149.4 1.6 %copy-done = f32[256,2,8,128]{3,2,1,0:T(8,128)S(1)} copy-done((f32[256,2,8,128]{3,2,1,0:T(8,128)S(1)}, f32[256,2,8,128]{3,2,1,0:T(8,128)}, u32[]{:S(2)}) %copy-start) | copy-done | bytes 2097176
  151.0 0.0 copy-start.1
  151.0 2.8 %shard_map.104 = (f32[27,96,96]{2,1,0:T(8,128)}, f32[27,96,96]{2,1,0:T(8,128)}) custom-call(f32[256,2,8,128]{3,2,1,0:T(8,128)S(1)} %copy-done), custom_call_target="tpu_custom_call" | custom-call | tf_op jit(solution)/shard_map/pallas_call | solution.py:512
  153.8 0.0 copy-done.1
  153.8 0.9 copy.13
Async XLA Ops:
  149.4 1.6 %copy-start = (f32[256,2,8,128]{3,2,1,0:T(8,128)S(1)}, f32[256,2,8,128]{3,2,1,0:T(8,128)}, u32[]{:S(2)}) copy-start(f32[256,2,8,128]{3,2,1,0:T(8,128)} %get-tuple-element.8.p_ref) | copy-start | bytes 6291460
  151.0 2.8 %copy-start.1 = (bf16[32,96,128]{2,1,0:T(8,128)(2,1)S(1)}, bf16[32,96,128]{2,1,0:T(8,128)(2,1)}, u32[]{:S(2)}) copy-start(bf16[32,96,128]{2,1,0:T(8,128)(2,1)} %get-tuple-element.7) | copy-start | bytes 2359300

commit v2 on v1

v2 whole, which is shorter than its diff:
```python
import functools

import jax
import jax.numpy as jnp
from jax import lax
from jax.experimental import pallas as pl
from jax.experimental.pallas import tpu as pltpu
from jax.sharding import PartitionSpec as P

MESH = pl.DeviceIdType.MESH
F32 = jnp.float32
BF16 = jnp.bfloat16
epsilon = 1e-06

FRAMES = 16
TILES = 16
CLIPS = 16
C = 96
W = 128
TAPS = 9 * C
PADDED = 896
UNROLL = 2
EARLY = 4


def inverse_rms(x):
    return lax.rsqrt(jnp.mean(x * x, axis=0, keepdims=True) + epsilon)


def sigmoid(u):
    return 0.5 * jnp.tanh(0.5 * u) + 0.5


def norm_silu(x, gain):
    u = gain * (x * inverse_rms(x))
    return u * sigmoid(u)


def norm_backward(g, x, gain):
    r = inverse_rms(x)
    normed = x * r
    u = gain * normed
    sig = sigmoid(u)
    q = g * gain * sig * (1.0 + u * (1.0 - sig))
    p = jnp.mean(q * normed, axis=0, keepdims=True)
    return r * (q - normed * p)


def mid_both(g, x, gain):
    r = inverse_rms(x)
    normed = x * r
    u = gain * normed
    sig = sigmoid(u)
    q = g * gain * sig * (1.0 + u * (1.0 - sig))
    p = jnp.mean(q * normed, axis=0, keepdims=True)
    return u * sig, r * (q - normed * p)


def put_row(y_ref, f, r, value):
    lane = lax.broadcasted_iota(jnp.int32, (C, W), 1)
    wide = value.astype(F32)
    low = jnp.where(lane == 0, 0.0, pltpu.roll(wide, 1, 1)).astype(BF16)
    high = jnp.where(lane == W - 1, 0.0, pltpu.roll(wide, W - 1, 1)).astype(BF16)
    for e, v in enumerate((low, value, high)):
        for b in range(3):
            h = r - b
            if 0 <= h < 2:
                y_ref[f, (b * 3 + e) * C:(b * 3 + e + 1) * C, h * W:(h + 1) * W] = v


def kernel(
    x_ref, rw_ref, own_ref, scored_ref, g1_ref, g2_ref, k1_ref, k2_ref,
    out_ref, res_ref,
    rin, rrw, k1f, k1t, k2t, g1c, g2c, pick,
    x4, xg4, xh4, yin, yg, yh, gm, act, gh, c1, c2, fb,
    w, bb, sb, r0, s1b, r1, c16, r2,
    in_s, in_r, rw_s, rw_r, loc, halo_s, halo_r, f_s, f_r,
    s0_s, s0_r, s1_s, s1_r, s2_s, s2_r, a1_s, a1_r, a0_s, a0_r,
):
    clip = lax.axis_index("clip")
    me = lax.axis_index("tile")
    core = me % 2
    z = me // 2
    sibling = me + 1 - 2 * core

    def tile_peer(i):
        step = i // 2 + 1
        return (me + (1 - i % 2) * step + (i % 2) * (TILES - step)) % TILES

    def clip_peer(i):
        return (clip + i + 1) % CLIPS

    def z_of(i):
        return (z + i + 1) % 8

    def loop(n, body):
        def step(i, carry):
            body(i)
            return carry

        lax.fori_loop(0, n, step, 0)

    barrier = pltpu.get_barrier_semaphore()
    loop(15, lambda i: pl.semaphore_signal(
        barrier, inc=1, device_id=(clip, tile_peer(i)), device_id_type=MESH))
    loop(15, lambda i: pl.semaphore_signal(
        barrier, inc=1, device_id=(clip_peer(i), me), device_id_type=MESH))

    def column(row, n, zero):
        eye = (lax.broadcasted_iota(jnp.int32, (n, n), 0)
               == lax.broadcasted_iota(jnp.int32, (n, n), 1))
        return jnp.sum(jnp.where(eye, jnp.broadcast_to(row, (n, n)), zero), axis=1, keepdims=True)

    g1c[...] = jnp.broadcast_to(column(g1_ref[...], C, 0.0), (C, W))
    g2c[...] = jnp.broadcast_to(column(g2_ref[...], C, 0.0), (C, W))

    own_row = own_ref[...]
    own_col = column(own_row, 16, 0)
    earlier = (lax.broadcasted_iota(jnp.int32, (16, 16), 1)
               < lax.broadcasted_iota(jnp.int32, (16, 16), 0))
    same = own_col == own_row
    ranking = jnp.sum(jnp.where(same & earlier, 1, 0), axis=1, keepdims=True)
    slot = own_col * 2 + ranking
    by_slot = jnp.where(
        slot == lax.shift_right_logical(lax.broadcasted_iota(jnp.int32, (16, 512), 1), 4),
        1.0, 0.0)
    by_frame = jnp.where(
        scored_ref[...]
        == lax.shift_right_logical(lax.broadcasted_iota(jnp.int32, (256, 16), 0), 4),
        1.0, 0.0)
    table = jnp.dot(by_frame, by_slot, preferred_element_type=F32)
    row16 = lax.broadcasted_iota(jnp.int32, (256, 512), 0) & 15
    col16 = lax.broadcasted_iota(jnp.int32, (256, 512), 1) & 15
    pick[...] = jnp.where(row16 == col16, table, 0.0).astype(BF16)

    for a in range(3):
        rows = slice(a * C, (a + 1) * C)
        k1f[rows, :] = jnp.concatenate(
            [k1_ref[a * 9 + i].astype(F32) for i in range(9)], axis=1).astype(BF16)
        k1t[rows, :] = jnp.transpose(jnp.concatenate(
            [k1_ref[a * 9 + 8 - i] for i in range(9)], axis=0).astype(F32)).astype(BF16)
        k2t[rows, :] = jnp.transpose(jnp.concatenate(
            [k2_ref[a * 9 + 8 - i] for i in range(9)], axis=0).astype(F32)).astype(BF16)

    act[0:2] = jnp.zeros((2, C, 2 * W), BF16)
    gh[16:18] = jnp.zeros((2, C, 2 * W), BF16)
    w[...] = jnp.zeros_like(w)
    for n in range(2):
        bb[n, 126:128] = jnp.zeros((2, 16, 128), F32)
        sb[n, 126:128] = jnp.zeros((2, 16, 128), BF16)

    pl.semaphore_wait(barrier, 30)

    def in_copy(src, dst, slot, peer):
        return pltpu.make_async_remote_copy(
            src_ref=x_ref.at[pl.ds(2 * src, 2)], dst_ref=rin.at[dst],
            send_sem=in_s.at[src], recv_sem=in_r.at[slot],
            device_id=(clip, peer), device_id_type=MESH)

    def rw_copy(src, dst, slot, peer):
        return pltpu.make_async_remote_copy(
            src_ref=rw_ref.at[:, pl.ds(2 * src, 2)], dst_ref=rrw.at[dst],
            send_sem=rw_s.at[src], recv_sem=rw_r.at[slot],
            device_id=(clip, peer), device_id_type=MESH)

    own_in = pltpu.make_async_copy(x_ref.at[pl.ds(2 * me, 2)], rin.at[me], loc.at[0])
    own_rw = pltpu.make_async_copy(rw_ref.at[:, pl.ds(2 * me, 2)], rrw.at[me], loc.at[1])

    def start_in(i):
        peer = tile_peer(14 - i)
        in_copy(peer, me, me, peer).start()

    def start_rw(i):
        peer = tile_peer(14 - i)
        rw_copy(peer, me, me, peer).start()

    loop(15, start_rw)
    own_rw.start()
    loop(EARLY, start_in)
    own_in.start()

    low_peer, high_peer = (me + TILES - 1) % TILES, (me + 1) % TILES

    def halo_pair(ref, k):
        up = pltpu.make_async_remote_copy(
            src_ref=ref.at[2], dst_ref=ref.at[0],
            send_sem=halo_s.at[2 * k], recv_sem=halo_r.at[2 * k],
            device_id=(clip, high_peer), device_id_type=MESH)
        down = pltpu.make_async_remote_copy(
            src_ref=ref.at[1], dst_ref=ref.at[3],
            send_sem=halo_s.at[2 * k + 1], recv_sem=halo_r.at[2 * k + 1],
            device_id=(clip, low_peer), device_id_type=MESH)
        return up, down

    def put_halo(ref, y_ref):
        def body(f):
            put_row(y_ref, f, 0, jnp.where(me > 0, ref[0, f].astype(F32), 0.0).astype(BF16))
            put_row(y_ref, f, 3, jnp.where(me < TILES - 1, ref[3, f].astype(F32), 0.0).astype(BF16))

        loop(FRAMES, body)

    def rw_arrived(i):
        src = tile_peer(i)
        rw_copy(src, src, src, src).wait_recv()

    own_rw.wait()
    loop(15, rw_arrived)
    for i in range(C // 16):
        rows = slice(16 * i, 16 * i + 16)
        slots = jnp.concatenate(
            [rrw[:, :, h, rows, :].reshape(512, W) for h in range(2)], axis=1)
        got = jnp.dot(pick[...], slots, preferred_element_type=F32).astype(BF16)
        got = got.reshape(FRAMES, 16, 2 * W)
        xg4[1, :, rows, :] = got[:, :, :W]
        xg4[2, :, rows, :] = got[:, :, W:]
    halo = halo_pair(xg4, 0)
    for copy in halo:
        copy.start()
    loop(15 - EARLY, lambda i: start_in(i + EARLY))

    def put_own(f):
        for h in range(2):
            put_row(yg, f, 1 + h, xg4[1 + h, f])

    loop(FRAMES, put_own)
    for copy in halo:
        copy.wait()
    put_halo(xg4, yg)

    def conv(kernel_ref, y_ref, first, reverse, each):
        c1[...] = jnp.zeros_like(c1)
        c2[...] = jnp.zeros_like(c2)

        def frame(f, one, two):
            p = jnp.dot(kernel_ref[...], y_ref[f], preferred_element_type=F32)
            if first is not None:
                one, two = jnp.where(f == FRAMES - 1, 0.0, one), jnp.where(f == FRAMES - 1, 0.0, two)
            return p[2 * C:] + one, p[C:2 * C] + two, p[:C]

        if first is not None:
            zero = jnp.zeros((C, 2 * W), F32)
            _, one, two = frame((first + 2) % FRAMES, zero, zero)
            _, one, two = frame((first + 1) % FRAMES, one, two)
            c1[...] = one
            c2[...] = two

        def body(i):
            one, two = c1[...], c2[...]
            for k in range(UNROLL):
                f = i * UNROLL + k
                if first is not None:
                    f = (first + FRAMES - f) % FRAMES
                elif reverse:
                    f = FRAMES - 1 - f
                value, one, two = frame(f, one, two)
                each(f, value.astype(BF16))
            c1[...] = one
            c2[...] = two

        loop(FRAMES // UNROLL, body)

    def keep(f, g):
        gm[f] = g

    conv(k2t, yg, None, True, keep)

    def first(f):
        for h in range(2):
            v = norm_silu(rin[f, h].astype(F32), g1c[...]).astype(BF16)
            x4[1 + h, f] = v
            put_row(yin, f, 1 + h, v)

    own_in.wait()
    first(me)

    def arrived(i):
        src = tile_peer(i)
        in_copy(src, src, src, src).wait_recv()
        first(src)

    loop(15, arrived)
    halo = halo_pair(x4, 1)
    for copy in halo:
        copy.start()
    for copy in halo:
        copy.wait()
    put_halo(x4, yin)

    def mid(f, h):
        for row in range(2):
            lanes = slice(row * W, (row + 1) * W)
            v, g = mid_both(gm[f, :, lanes].astype(F32), h[:, lanes].astype(F32), g2c[...])
            act[f + 2, :, lanes] = v.astype(BF16)
            g = g.astype(BF16)
            xh4[1 + row, f] = g
            gh[f, :, lanes] = g
            put_row(yh, f, 1 + row, g)

    conv(k1f, yin, None, False, mid)
    halo = halo_pair(xh4, 2)
    for copy in halo:
        copy.start()

    mine, other = core * 64, (1 - core) * 64
    base = mine + 4 * clip

    def weight(n, left, y_ref):
        def body(i):
            total = w[n, :, :TAPS]
            for k in range(4):
                f = i * 4 + k
                rows = left(f)
                total = total + lax.dot_general(
                    rows, y_ref[f], (((1,), (1,)), ((), ())), preferred_element_type=F32)
            w[n, :, :TAPS] = total

        loop(FRAMES // 4, body)

        def pack(i):
            rows = w[n, pl.ds(pl.multiple_of(16 * i, 16), 16), :]
            for j in range(7):
                piece = rows[:, 128 * j:128 * (j + 1)]
                bb[n, 7 * i + j] = piece
                sb[n, 7 * i + j] = piece.astype(BF16)

        loop(18, pack)

    def s0_copy(n):
        return pltpu.make_async_remote_copy(
            src_ref=sb.at[n, pl.ds(other, 64)], dst_ref=r0.at[n],
            send_sem=s0_s.at[n], recv_sem=s0_r.at[n],
            device_id=(clip, sibling), device_id_type=MESH)

    def s1_copy(n, piece, slot_at, peer):
        return pltpu.make_async_remote_copy(
            src_ref=s1b.at[n, pl.ds(4 * piece, 4)], dst_ref=r1.at[n, slot_at],
            send_sem=s1_s.at[n, piece], recv_sem=s1_r.at[n, slot_at],
            device_id=(peer, me), device_id_type=MESH)

    def s2_copy(n, to, slot_at):
        return pltpu.make_async_remote_copy(
            src_ref=c16.at[n], dst_ref=r2.at[n, slot_at],
            send_sem=s2_s.at[n, to], recv_sem=s2_r.at[n, slot_at],
            device_id=(clip, 2 * to + core), device_id_type=MESH)

    def a1_copy(n, at, to):
        piece = res_ref.at[n, pl.ds(mine + 4 * at, 4)]
        return pltpu.make_async_remote_copy(
            src_ref=piece, dst_ref=piece,
            send_sem=a1_s.at[n, to], recv_sem=a1_r.at[n, at],
            device_id=(to, me), device_id_type=MESH)

    def a0_copy(n, half):
        piece = res_ref.at[n, pl.ds(half, 64)]
        return pltpu.make_async_remote_copy(
            src_ref=piece, dst_ref=piece, send_sem=a0_s.at[n], recv_sem=a0_r.at[n],
            device_id=(clip, sibling), device_id_type=MESH)

    def sum_pair(n):
        s0_copy(n).start()

    def sum_clips(n):
        s0_copy(n).wait()

        def add(i):
            at = pl.ds(4 * i, 4)
            s1b[n, at] = (
                bb[n, pl.ds(mine + 4 * i, 4)] + r0[n, at].astype(F32)).astype(BF16)

        loop(16, add)
        loop(15, lambda i: s1_copy(n, clip_peer(i), clip, clip_peer(i)).start())
        r1[n, clip] = s1b[n, pl.ds(4 * clip, 4)]

    def sum_z(n):
        loop(15, lambda i: s1_copy(n, clip_peer(i), clip_peer(i), clip_peer(i)).wait())

        def add(i):
            total = r1[n, 0, i].astype(F32)
            for p in range(1, CLIPS):
                total = total + r1[n, p, i].astype(F32)
            c16[n, i] = total.astype(BF16)

        loop(4, add)
        loop(7, lambda i: s2_copy(n, z_of(i), z).start())
        r2[n, z] = c16[n]

    def spread_clips(n):
        loop(7, lambda i: s2_copy(n, z_of(i), z_of(i)).wait())
        total = r2[n, 0].astype(F32)
        for p in range(1, 8):
            total = total + r2[n, p].astype(F32)
        res_ref[n, pl.ds(base, 4)] = total.astype(BF16)
        loop(15, lambda i: a1_copy(n, clip, clip_peer(i)).start())

    def spread_pair(n):
        def finish(i):
            a1_copy(n, clip_peer(i), clip_peer(i)).wait_recv()
            a1_copy(n, clip, clip_peer(i)).wait_send()

        loop(15, finish)
        a0_copy(n, mine).start()

    def finish_sum(n):
        a0_copy(n, other).wait_recv()
        a0_copy(n, mine).wait_send()

    weight(0, lambda f: jnp.concatenate([gh[f + 2], gh[f + 1], gh[f]], axis=0), yin)
    sum_pair(0)
    weight(1, lambda f: jnp.concatenate([act[f], act[f + 1], act[f + 2]], axis=0), yg)
    sum_pair(1)
    sum_clips(0)

    for copy in halo:
        copy.wait()
    put_halo(xh4, yh)
    sum_clips(1)

    def f_copy(f, dst_rows, slot_at, peer):
        return pltpu.make_async_remote_copy(
            src_ref=fb.at[f], dst_ref=out_ref.at[pl.ds(2 * dst_rows, 2)],
            send_sem=f_s.at[f], recv_sem=f_r.at[slot_at],
            device_id=(clip, peer), device_id_type=MESH)

    own_out = pltpu.make_async_copy(fb.at[me], out_ref.at[pl.ds(2 * me, 2)], loc.at[2])

    def back_in(f, g):
        for row in range(2):
            v = norm_backward(
                g[:, row * W:(row + 1) * W].astype(F32), rin[f, row].astype(F32), g1c[...])
            fb[f, row] = (xg4[1 + row, f].astype(F32) + v).astype(BF16)

        @pl.when(f != me)
        def _():
            f_copy(f, me, me, f).start()

        @pl.when(f == me)
        def _():
            own_out.start()

    conv(k1t, yh, (me + 8) % FRAMES, True, back_in)

    sum_z(0)
    sum_z(1)
    spread_clips(0)
    spread_clips(1)
    spread_pair(0)
    spread_pair(1)
    finish_sum(0)
    finish_sum(1)

    own_out.wait()

    def drain(i):
        peer = tile_peer(i)
        f_copy(peer, peer, peer, peer).wait_recv()
        f_copy(peer, me, me, peer).wait_send()
        in_copy(peer, me, me, peer).wait_send()
        rw_copy(peer, me, me, peer).wait_send()

    loop(15, drain)


def unpack(scale, p_ref, o1_ref, o2_ref, s_ref):
    for n, o_ref in enumerate((o1_ref, o2_ref)):
        def body(i, carry):
            for j in range(7):
                s_ref[pl.ds(pl.multiple_of(16 * i, 16), 16), 128 * j:128 * (j + 1)] = (
                    p_ref[n, 7 * i + j].astype(F32) * scale)
            return carry

        lax.fori_loop(0, 18, body, 0)
        for a in range(3):
            for i in range(9):
                block = s_ref[a * C:(a + 1) * C, i * C:(i + 1) * C]
                if n == 0:
                    o_ref[a * 9 + i] = block
                else:
                    o_ref[a * 9 + 8 - i] = jnp.transpose(block)


def local(
    decoder_input, reward_grad, reward_owner, scored_frame,
    first_gain, second_gain, first_kernel, second_kernel,
):
    vmem = pl.BlockSpec(memory_space=pltpu.VMEM)
    hbm = pl.BlockSpec(memory_space=pl.ANY)
    dma = pltpu.SemaphoreType.DMA
    feature, packed = pl.pallas_call(
        kernel,
        out_shape=(
            jax.ShapeDtypeStruct((32, C, W), BF16),
            jax.ShapeDtypeStruct((2, 128, 16, 128), BF16),
        ),
        in_specs=[hbm, hbm] + [vmem] * 6,
        out_specs=(hbm, vmem),
        scratch_shapes=[
            pltpu.VMEM((16, 2, C, W), BF16),
            pltpu.VMEM((16, 2, 2, C, W), BF16),
            pltpu.VMEM((3 * C, TAPS), BF16),
            pltpu.VMEM((3 * C, TAPS), BF16),
            pltpu.VMEM((3 * C, TAPS), BF16),
            pltpu.VMEM((C, W), F32),
            pltpu.VMEM((C, W), F32),
            pltpu.VMEM((256, 512), BF16),
            pltpu.VMEM((4, 16, C, W), BF16),
            pltpu.VMEM((4, 16, C, W), BF16),
            pltpu.VMEM((4, 16, C, W), BF16),
            pltpu.VMEM((16, TAPS, 2 * W), BF16),
            pltpu.VMEM((16, TAPS, 2 * W), BF16),
            pltpu.VMEM((16, TAPS, 2 * W), BF16),
            pltpu.VMEM((16, C, 2 * W), BF16),
            pltpu.VMEM((18, C, 2 * W), BF16),
            pltpu.VMEM((18, C, 2 * W), BF16),
            pltpu.VMEM((C, 2 * W), F32),
            pltpu.VMEM((C, 2 * W), F32),
            pltpu.VMEM((16, 2, C, W), BF16),
            pltpu.VMEM((2, 3 * C, PADDED), F32),
            pltpu.VMEM((2, 128, 16, 128), F32),
            pltpu.VMEM((2, 128, 16, 128), BF16),
            pltpu.VMEM((2, 64, 16, 128), BF16),
            pltpu.VMEM((2, 64, 16, 128), BF16),
            pltpu.VMEM((2, 16, 4, 16, 128), BF16),
            pltpu.VMEM((2, 4, 16, 128), BF16),
            pltpu.VMEM((2, 8, 4, 16, 128), BF16),
            dma((16,)), dma((16,)), dma((16,)), dma((16,)), dma((3,)),
            dma((6,)), dma((6,)), dma((16,)), dma((16,)),
            dma((2,)), dma((2,)), dma((2, 16)), dma((2, 16)), dma((2, 8)), dma((2, 8)),
            dma((2, 16)), dma((2, 16)), dma((2,)), dma((2,)),
        ],
        compiler_params=pltpu.CompilerParams(
            collective_id=0, has_side_effects=True, vmem_limit_bytes=60 * 2**20),
    )(
        decoder_input[0, 0],
        reward_grad[0],
        reward_owner[0].reshape(1, 16),
        scored_frame,
        first_gain.reshape(1, C),
        second_gain.reshape(1, C),
        first_kernel.reshape(27, C, C),
        second_kernel.reshape(27, C, C),
    )
    first_total, second_total = pl.pallas_call(
        functools.partial(unpack, 1.0 / 1024.0),
        out_shape=(jax.ShapeDtypeStruct((27, C, C), F32),) * 2,
        in_specs=[vmem],
        out_specs=(vmem, vmem),
        scratch_shapes=[pltpu.VMEM((3 * C, PADDED), F32)],
        compiler_params=pltpu.CompilerParams(vmem_limit_bytes=32 * 2**20),
    )(packed)
    shape = (3, 3, 3, C, C)
    return feature[None, None], first_total.reshape(shape), second_total.reshape(shape)


def solution(mesh):
    in_specs = (
        P("clip", "tile", None, None, None),
        P("clip", "tile", None, None, None),
        P("clip", None, None),
        P("clip", None),
        P(),
        P(),
        P(),
        P(),
    )
    out_specs = (P("clip", "tile", None, None, None), P(), P())
    return jax.shard_map(local, mesh=mesh, in_specs=in_specs, out_specs=out_specs, check_vma=False)
```

time: 155 us -> 139 us (0.90)
  Pallas kernels: 150 us -> 136 us
  local copies, waits for them, and re-layouts: 3.8 us -> 2.1 us
    pallas_call x1, Pallas kernels: 147 us -> 134 us  [local(): pl.pallas_call(kernel, out_shape=(jax.ShapeDtypeStruct((32, C, W), BF16),...]
where the time goes in v2:
time: 139 us
  Pallas kernels  136 us (98%)
  local copies, waits for them, and re-layouts  2.1 us (2%)
    pallas_call x1, Pallas kernels, local(): pl.pallas_call(kernel, out_shape=(jax.ShapeDtypeStruct((32, C, W), BF16),...  134 us

profile of v2, /device:TPU:1, one launch (start us, length us, event | category | flops | bytes accessed | tf_op | source)
XLA Modules:
  0.0 139.2 jit_solution(14627185782981233296)
XLA Ops:
  0.6 133.8 %shard_map.103 = (bf16[32,96,128]{2,1,0:T(8,128)(2,1)}, bf16[2,128,16,128]{3,2,1,0:T(8,128)(2,1)}) custom-call(bf16[32,96,128]{2,1,0:T(8,128)(2,1)} %bitcast.12, bf16[2,32,96,128]{3,2,1,0:T(8,128)(2,1)} %bitcast.10, s32[1,16]{1,0:T(1,128)} %bitcast.15, s32[1,16]{1,0:T(1,128)} %scored_ref.1, f32[1,96]{1,0:T(1,128)} %bitcast.16, f32[1,96]{1,0:T(1,128)} %bitcast.17, ...), custom_call_target="tpu_custom_call" | custom-call | tf_op jit(solution)/shard_map/pallas_call | solution.py:488
  134.5 0.0 copy-start
  134.5 1.2 copy-done
  135.7 0.0 copy-start.1
  135.7 2.6 %shard_map.104 = (f32[27,96,96]{2,1,0:T(8,128)}, f32[27,96,96]{2,1,0:T(8,128)}) custom-call(bf16[2,128,16,128]{3,2,1,0:T(8,128)(2,1)S(1)} %copy-done), custom_call_target="tpu_custom_call" | custom-call | tf_op jit(solution)/shard_map/pallas_call | solution.py:542
  138.3 0.0 copy-done.1
  138.3 0.9 copy.12
Async XLA Ops:
  134.5 1.2 copy-start
  135.7 2.6 %copy-start.1 = (bf16[32,96,128]{2,1,0:T(8,128)(2,1)S(1)}, bf16[32,96,128]{2,1,0:T(8,128)(2,1)}, u32[]{:S(2)}) copy-start(bf16[32,96,128]{2,1,0:T(8,128)(2,1)} %get-tuple-element.7) | copy-start | bytes 2359300

commit v3 on v2

--- a/solution.py
+++ b/solution.py
@@ -20,7 +20,9 @@
 TAPS = 9 * C
 PADDED = 896
 UNROLL = 2
-EARLY = 4
+EARLY = 15
+HELD = 10
+CHUNK = 4
 
 
 def inverse_rms(x):
@@ -74,7 +76,7 @@
     rin, rrw, k1f, k1t, k2t, g1c, g2c, pick,
     x4, xg4, xh4, yin, yg, yh, gm, act, gh, c1, c2, fb,
     w, bb, sb, r0, s1b, r1, c16, r2,
-    in_s, in_r, rw_s, rw_r, loc, halo_s, halo_r, f_s, f_r,
+    in_s, in_r, rw_s, rw_r, loc, halo_s, halo_r, x_s, x_r, f_s, f_r,
     s0_s, s0_r, s1_s, s1_r, s2_s, s2_r, a1_s, a1_r, a0_s, a0_r,
 ):
     clip = lax.axis_index("clip")
@@ -192,12 +194,21 @@
             device_id=(clip, low_peer), device_id_type=MESH)
         return up, down
 
-    def put_halo(ref, y_ref):
-        def body(f):
-            put_row(y_ref, f, 0, jnp.where(me > 0, ref[0, f].astype(F32), 0.0).astype(BF16))
-            put_row(y_ref, f, 3, jnp.where(me < TILES - 1, ref[3, f].astype(F32), 0.0).astype(BF16))
-
-        loop(FRAMES, body)
+    def put_halo(ref, y_ref, f):
+        put_row(y_ref, f, 0, jnp.where(me > 0, ref[0, f].astype(F32), 0.0).astype(BF16))
+        put_row(y_ref, f, 3, jnp.where(me < TILES - 1, ref[3, f].astype(F32), 0.0).astype(BF16))
+
+    def x_pair(c):
+        at = pl.ds(CHUNK * c, CHUNK)
+        up = pltpu.make_async_remote_copy(
+            src_ref=x4.at[2, at], dst_ref=x4.at[0, at],
+            send_sem=x_s.at[2 * c], recv_sem=x_r.at[2 * c],
+            device_id=(clip, high_peer), device_id_type=MESH)
+        down = pltpu.make_async_remote_copy(
+            src_ref=x4.at[1, at], dst_ref=x4.at[3, at],
+            send_sem=x_s.at[2 * c + 1], recv_sem=x_r.at[2 * c + 1],
+            device_id=(clip, low_peer), device_id_type=MESH)
+        return up, down
 
     def rw_arrived(i):
         src = tile_peer(i)
@@ -223,11 +234,8 @@
             put_row(yg, f, 1 + h, xg4[1 + h, f])
 
     loop(FRAMES, put_own)
-    for copy in halo:
-        copy.wait()
-    put_halo(xg4, yg)
-
-    def conv(kernel_ref, y_ref, first, reverse, each):
+
+    def conv(kernel_ref, y_ref, first, each):
         c1[...] = jnp.zeros_like(c1)
         c2[...] = jnp.zeros_like(c2)
 
@@ -247,22 +255,21 @@
         def body(i):
             one, two = c1[...], c2[...]
             for k in range(UNROLL):
-                f = i * UNROLL + k
+                step = i * UNROLL + k
+                f = step
                 if first is not None:
                     f = (first + FRAMES - f) % FRAMES
-                elif reverse:
+                else:
                     f = FRAMES - 1 - f
                 value, one, two = frame(f, one, two)
-                each(f, value.astype(BF16))
+                each(step, f, value.astype(BF16))
             c1[...] = one
             c2[...] = two
 
         loop(FRAMES // UNROLL, body)
 
-    def keep(f, g):
+    def keep(step, f, g):
         gm[f] = g
-
-    conv(k2t, yg, None, True, keep)
 
     def first(f):
         for h in range(2):
@@ -279,12 +286,17 @@
         first(src)
 
     loop(15, arrived)
-    halo = halo_pair(x4, 1)
-    for copy in halo:
-        copy.start()
+
+    def send_x(c):
+        for copy in x_pair(c):
+            copy.start()
+
+    loop(FRAMES // CHUNK, send_x)
+
     for copy in halo:
         copy.wait()
-    put_halo(x4, yin)
+    loop(FRAMES, lambda f: put_halo(xg4, yg, f))
+    conv(k2t, yg, None, keep)
 
     def mid(f, h):
         for row in range(2):
@@ -296,13 +308,30 @@
             gh[f, :, lanes] = g
             put_row(yh, f, 1 + row, g)
 
-    conv(k1f, yin, None, False, mid)
-    halo = halo_pair(xh4, 2)
+    c1[...] = jnp.zeros_like(c1)
+    c2[...] = jnp.zeros_like(c2)
+
+    def chunk(c):
+        for copy in x_pair(c):
+            copy.wait()
+        for k in range(CHUNK):
+            put_halo(x4, yin, c * CHUNK + k)
+        one, two = c1[...], c2[...]
+        for k in range(CHUNK):
+            f = c * CHUNK + k
+            p = jnp.dot(k1f[...], yin[f], preferred_element_type=F32)
+            mid(f, (p[2 * C:] + one).astype(BF16))
+            one = p[C:2 * C] + two
+            two = p[:C]
+        c1[...] = one
+        c2[...] = two
+
+    loop(FRAMES // CHUNK, chunk)
+    halo = halo_pair(xh4, 1)
     for copy in halo:
         copy.start()
 
     mine, other = core * 64, (1 - core) * 64
-    base = mine + 4 * clip
 
     def weight(n, left, y_ref):
         def body(i):
@@ -325,10 +354,10 @@
 
         loop(18, pack)
 
-    def s0_copy(n):
-        return pltpu.make_async_remote_copy(
-            src_ref=sb.at[n, pl.ds(other, 64)], dst_ref=r0.at[n],
-            send_sem=s0_s.at[n], recv_sem=s0_r.at[n],
+    def s0_copy(n, piece):
+        return pltpu.make_async_remote_copy(
+            src_ref=sb.at[n, pl.ds(other + 4 * piece, 4)], dst_ref=r0.at[n, pl.ds(4 * piece, 4)],
+            send_sem=s0_s.at[n, piece], recv_sem=s0_r.at[n, piece],
             device_id=(clip, sibling), device_id_type=MESH)
 
     def s1_copy(n, piece, slot_at, peer):
@@ -337,82 +366,86 @@
             send_sem=s1_s.at[n, piece], recv_sem=s1_r.at[n, slot_at],
             device_id=(peer, me), device_id_type=MESH)
 
-    def s2_copy(n, to, slot_at):
-        return pltpu.make_async_remote_copy(
-            src_ref=c16.at[n], dst_ref=r2.at[n, slot_at],
-            send_sem=s2_s.at[n, to], recv_sem=s2_r.at[n, slot_at],
+    def s2_copy(to, slot_at):
+        return pltpu.make_async_remote_copy(
+            src_ref=c16, dst_ref=r2.at[slot_at],
+            send_sem=s2_s.at[to], recv_sem=s2_r.at[slot_at],
             device_id=(clip, 2 * to + core), device_id_type=MESH)
 
-    def a1_copy(n, at, to):
-        piece = res_ref.at[n, pl.ds(mine + 4 * at, 4)]
+    def a1_copy(at, to):
+        piece = res_ref.at[16 * core + at]
         return pltpu.make_async_remote_copy(
             src_ref=piece, dst_ref=piece,
-            send_sem=a1_s.at[n, to], recv_sem=a1_r.at[n, at],
+            send_sem=a1_s.at[to], recv_sem=a1_r.at[at],
             device_id=(to, me), device_id_type=MESH)
 
-    def a0_copy(n, half):
-        piece = res_ref.at[n, pl.ds(half, 64)]
-        return pltpu.make_async_remote_copy(
-            src_ref=piece, dst_ref=piece, send_sem=a0_s.at[n], recv_sem=a0_r.at[n],
+    def a0_copy(half, at):
+        piece = res_ref.at[16 * half + at]
+        return pltpu.make_async_remote_copy(
+            src_ref=piece, dst_ref=piece, send_sem=a0_s.at[at], recv_sem=a0_r.at[at],
             device_id=(clip, sibling), device_id_type=MESH)
 
     def sum_pair(n):
-        s0_copy(n).start()
+        loop(16, lambda i: s0_copy(n, clip_peer(i)).start())
 
     def sum_clips(n):
-        s0_copy(n).wait()
+        def piece_of(p):
+            s0_copy(n, p).wait()
+            return (bb[n, pl.ds(mine + 4 * p, 4)]
+                    + r0[n, pl.ds(4 * p, 4)].astype(F32)).astype(BF16)
 
         def add(i):
-            at = pl.ds(4 * i, 4)
-            s1b[n, at] = (
-                bb[n, pl.ds(mine + 4 * i, 4)] + r0[n, at].astype(F32)).astype(BF16)
-
-        loop(16, add)
-        loop(15, lambda i: s1_copy(n, clip_peer(i), clip, clip_peer(i)).start())
-        r1[n, clip] = s1b[n, pl.ds(4 * clip, 4)]
-
-    def sum_z(n):
-        loop(15, lambda i: s1_copy(n, clip_peer(i), clip_peer(i), clip_peer(i)).wait())
-
-        def add(i):
-            total = r1[n, 0, i].astype(F32)
-            for p in range(1, CLIPS):
-                total = total + r1[n, p, i].astype(F32)
-            c16[n, i] = total.astype(BF16)
-
-        loop(4, add)
-        loop(7, lambda i: s2_copy(n, z_of(i), z).start())
-        r2[n, z] = c16[n]
-
-    def spread_clips(n):
-        loop(7, lambda i: s2_copy(n, z_of(i), z_of(i)).wait())
-        total = r2[n, 0].astype(F32)
+            p = clip_peer(i)
+            s1b[n, pl.ds(4 * p, 4)] = piece_of(p)
+            s1_copy(n, p, clip, p).start()
+
+        loop(15, add)
+        r1[n, clip] = piece_of(clip)
+
+    def sum_z():
+        for n in range(2):
+            loop(15, lambda i: s1_copy(n, clip_peer(i), clip_peer(i), clip_peer(i)).wait())
+
+            def add(i):
+                total = r1[n, 0, i].astype(F32)
+                for p in range(1, CLIPS):
+                    total = total + r1[n, p, i].astype(F32)
+                c16[4 * n + i] = total.astype(BF16)
+
+            loop(4, add)
+        loop(7, lambda i: s2_copy(z_of(i), z).start())
+        r2[z] = c16[...]
+
+    def spread_clips():
+        loop(7, lambda i: s2_copy(z_of(i), z_of(i)).wait())
+        total = r2[0].astype(F32)
         for p in range(1, 8):
-            total = total + r2[n, p].astype(F32)
-        res_ref[n, pl.ds(base, 4)] = total.astype(BF16)
-        loop(15, lambda i: a1_copy(n, clip, clip_peer(i)).start())
-
-    def spread_pair(n):
-        def finish(i):
-            a1_copy(n, clip_peer(i), clip_peer(i)).wait_recv()
-            a1_copy(n, clip, clip_peer(i)).wait_send()
-
-        loop(15, finish)
-        a0_copy(n, mine).start()
-
-    def finish_sum(n):
-        a0_copy(n, other).wait_recv()
-        a0_copy(n, mine).wait_send()
+            total = total + r2[p].astype(F32)
+        res_ref[16 * core + clip] = total.astype(BF16)
+        loop(15, lambda i: a1_copy(clip, clip_peer(i)).start())
+        a0_copy(core, clip).start()
+
+    def spread_pair():
+        def forward(i):
+            p = clip_peer(i)
+            a1_copy(p, p).wait_recv()
+            a0_copy(core, p).start()
+
+        loop(15, forward)
+
+    def finish_sum():
+        loop(15, lambda i: a1_copy(clip, clip_peer(i)).wait_send())
+        loop(16, lambda i: a0_copy(1 - core, i).wait_recv())
+        loop(16, lambda i: a0_copy(core, i).wait_send())
 
     weight(0, lambda f: jnp.concatenate([gh[f + 2], gh[f + 1], gh[f]], axis=0), yin)
     sum_pair(0)
     weight(1, lambda f: jnp.concatenate([act[f], act[f + 1], act[f + 2]], axis=0), yg)
     sum_pair(1)
-    sum_clips(0)
-
     for copy in halo:
         copy.wait()
-    put_halo(xh4, yh)
+    loop(FRAMES, lambda f: put_halo(xh4, yh, f))
+    sum_clips(0)
     sum_clips(1)
 
     def f_copy(f, dst_rows, slot_at, peer):
@@ -423,30 +456,35 @@
 
     own_out = pltpu.make_async_copy(fb.at[me], out_ref.at[pl.ds(2 * me, 2)], loc.at[2])
 
-    def back_in(f, g):
+    def back_in(step, f, g):
         for row in range(2):
             v = norm_backward(
                 g[:, row * W:(row + 1) * W].astype(F32), rin[f, row].astype(F32), g1c[...])
             fb[f, row] = (xg4[1 + row, f].astype(F32) + v).astype(BF16)
 
+        @pl.when((f != me) & (step < FRAMES - HELD))
+        def _():
+            f_copy(f, me, me, f).start()
+
+        @pl.when(f == me)
+        def _():
+            own_out.start()
+
+    conv(k1t, yh, (me + 8) % FRAMES, back_in)
+
+    sum_z()
+
+    def send_held(i):
+        f = (me + 8 + HELD - i) % FRAMES
+
         @pl.when(f != me)
         def _():
             f_copy(f, me, me, f).start()
 
-        @pl.when(f == me)
-        def _():
-            own_out.start()
-
-    conv(k1t, yh, (me + 8) % FRAMES, True, back_in)
-
-    sum_z(0)
-    sum_z(1)
-    spread_clips(0)
-    spread_clips(1)
-    spread_pair(0)
-    spread_pair(1)
-    finish_sum(0)
-    finish_sum(1)
+    loop(HELD, send_held)
+    spread_clips()
+    spread_pair()
+    finish_sum()
 
     own_out.wait()
 
@@ -465,7 +503,7 @@
         def body(i, carry):
             for j in range(7):
                 s_ref[pl.ds(pl.multiple_of(16 * i, 16), 16), 128 * j:128 * (j + 1)] = (
-                    p_ref[n, 7 * i + j].astype(F32) * scale)
+                    p_ref[(7 * i + j) // 4, 4 * n + (7 * i + j) % 4].astype(F32) * scale)
             return carry
 
         lax.fori_loop(0, 18, body, 0)
@@ -489,7 +527,7 @@
         kernel,
         out_shape=(
             jax.ShapeDtypeStruct((32, C, W), BF16),
-            jax.ShapeDtypeStruct((2, 128, 16, 128), BF16),
+            jax.ShapeDtypeStruct((32, 8, 16, 128), BF16),
         ),
         in_specs=[hbm, hbm] + [vmem] * 6,
         out_specs=(hbm, vmem),
@@ -520,12 +558,12 @@
             pltpu.VMEM((2, 64, 16, 128), BF16),
             pltpu.VMEM((2, 64, 16, 128), BF16),
             pltpu.VMEM((2, 16, 4, 16, 128), BF16),
-            pltpu.VMEM((2, 4, 16, 128), BF16),
-            pltpu.VMEM((2, 8, 4, 16, 128), BF16),
+            pltpu.VMEM((8, 16, 128), BF16),
+            pltpu.VMEM((8, 8, 16, 128), BF16),
             dma((16,)), dma((16,)), dma((16,)), dma((16,)), dma((3,)),
-            dma((6,)), dma((6,)), dma((16,)), dma((16,)),
-            dma((2,)), dma((2,)), dma((2, 16)), dma((2, 16)), dma((2, 8)), dma((2, 8)),
-            dma((2, 16)), dma((2, 16)), dma((2,)), dma((2,)),
+            dma((4,)), dma((4,)), dma((8,)), dma((8,)), dma((16,)), dma((16,)),
+            dma((2, 16)), dma((2, 16)), dma((2, 16)), dma((2, 16)), dma((8,)), dma((8,)),
+            dma((16,)), dma((16,)), dma((16,)), dma((16,)),
         ],
         compiler_params=pltpu.CompilerParams(
             collective_id=0, has_side_effects=True, vmem_limit_bytes=60 * 2**20),

time: 139 us -> 133 us (0.957)
  Pallas kernels: 136 us -> 130 us
    pallas_call x1, Pallas kernels: 134 us -> 126 us  [local(): pl.pallas_call(kernel, out_shape=(jax.ShapeDtypeStruct((32, C, W), BF16),...]
    pallas_call x1, Pallas kernels: 2.6 us -> 4.22 us  [local(): pl.pallas_call(functools.partial(unpack, 1.0 / 1024.0), out_shape=(jax.Sh...]
where the time goes in v3:
time: 133 us
  Pallas kernels  130 us (98%)
  local copies, waits for them, and re-layouts  2.1 us (2%)
    pallas_call x1, Pallas kernels, local(): pl.pallas_call(kernel, out_shape=(jax.ShapeDtypeStruct((32, C, W), BF16),...  126 us
    pallas_call x1, Pallas kernels, local(): pl.pallas_call(functools.partial(unpack, 1.0 / 1024.0), out_shape=(jax.Sh...  4.22 us

profile of v3, /device:TPU:1, one launch (start us, length us, event | category | flops | bytes accessed | tf_op | source)
XLA Modules:
  0.0 132.5 jit_solution(13445143704088866705)
XLA Ops:
  0.6 125.5 %shard_map.103 = (bf16[32,96,128]{2,1,0:T(8,128)(2,1)}, bf16[32,8,16,128]{3,2,1,0:T(8,128)(2,1)}) custom-call(bf16[32,96,128]{2,1,0:T(8,128)(2,1)} %bitcast.12, bf16[2,32,96,128]{3,2,1,0:T(8,128)(2,1)} %bitcast.10, s32[1,16]{1,0:T(1,128)} %bitcast.15, s32[1,16]{1,0:T(1,128)} %scored_ref.1, f32[1,96]{1,0:T(1,128)} %bitcast.16, f32[1,96]{1,0:T(1,128)} %bitcast.17, ...), custom_call_target="tpu_custom_call" | custom-call | tf_op jit(solution)/shard_map/pallas_call | solution.py:526
  126.2 0.0 copy-start
  126.2 1.2 copy-done
  127.4 0.0 copy-start.1
  127.4 4.2 %shard_map.104 = (f32[27,96,96]{2,1,0:T(8,128)}, f32[27,96,96]{2,1,0:T(8,128)}) custom-call(bf16[32,8,16,128]{3,2,1,0:T(8,128)(2,1)S(1)} %copy-done), custom_call_target="tpu_custom_call" | custom-call | tf_op jit(solution)/shard_map/pallas_call | solution.py:580
  131.6 0.0 copy-done.1
  131.6 0.9 copy.12
Async XLA Ops:
  126.2 1.2 copy-start
  127.4 4.2 %copy-start.1 = (bf16[32,96,128]{2,1,0:T(8,128)(2,1)S(1)}, bf16[32,96,128]{2,1,0:T(8,128)(2,1)}, u32[]{:S(2)}) copy-start(bf16[32,96,128]{2,1,0:T(8,128)(2,1)} %get-tuple-element.7) | copy-start | bytes 2359300

commit v4 on v3

--- a/solution.py
+++ b/solution.py
@@ -19,9 +19,9 @@
 W = 128
 TAPS = 9 * C
 PADDED = 896
-UNROLL = 2
+UNROLL = 4
 EARLY = 15
-HELD = 10
+HELD = 13
 CHUNK = 4
 
 
@@ -442,10 +442,10 @@
     sum_pair(0)
     weight(1, lambda f: jnp.concatenate([act[f], act[f + 1], act[f + 2]], axis=0), yg)
     sum_pair(1)
+    sum_clips(0)
     for copy in halo:
         copy.wait()
     loop(FRAMES, lambda f: put_halo(xh4, yh, f))
-    sum_clips(0)
     sum_clips(1)
 
     def f_copy(f, dst_rows, slot_at, peer):
@@ -500,13 +500,10 @@
 
 def unpack(scale, p_ref, o1_ref, o2_ref, s_ref):
     for n, o_ref in enumerate((o1_ref, o2_ref)):
-        def body(i, carry):
-            for j in range(7):
-                s_ref[pl.ds(pl.multiple_of(16 * i, 16), 16), 128 * j:128 * (j + 1)] = (
-                    p_ref[(7 * i + j) // 4, 4 * n + (7 * i + j) % 4].astype(F32) * scale)
-            return carry
-
-        lax.fori_loop(0, 18, body, 0)
+        for t in range(126):
+            i, j = divmod(t, 7)
+            s_ref[16 * i:16 * (i + 1), 128 * j:128 * (j + 1)] = (
+                p_ref[t // 4, 4 * n + t % 4].astype(F32) * scale)
         for a in range(3):
             for i in range(9):
                 block = s_ref[a * C:(a + 1) * C, i * C:(i + 1) * C]

time: 133 us -> 127 us (0.955)
  Pallas kernels: 130 us -> 123 us
    pallas_call x1, Pallas kernels: 126 us -> 120 us  [local(): pl.pallas_call(kernel, out_shape=(jax.ShapeDtypeStruct((32, C, W), BF16),...]
    pallas_call x1, Pallas kernels: 4.22 us -> 2.66 us  [local(): pl.pallas_call(functools.partial(unpack, 1.0 / 1024.0), out_shape=(jax.Sh...]
where the time goes in v4:
time: 127 us; the launch traced here: 126 us
  Pallas kernels  123 us (97%)
  local copies, waits for them, and re-layouts  2.1 us (2%)
    pallas_call x1, Pallas kernels, local(): pl.pallas_call(kernel, out_shape=(jax.ShapeDtypeStruct((32, C, W), BF16),...  120 us
    pallas_call x1, Pallas kernels, local(): pl.pallas_call(functools.partial(unpack, 1.0 / 1024.0), out_shape=(jax.Sh...  2.66 us

profile of v4, /device:TPU:1, one launch (start us, length us, event | category | flops | bytes accessed | tf_op | source)
XLA Modules:
  0.0 125.9 jit_solution(11513087397379447093)
XLA Ops:
  0.6 120.5 %shard_map.103 = (bf16[32,96,128]{2,1,0:T(8,128)(2,1)}, bf16[32,8,16,128]{3,2,1,0:T(8,128)(2,1)}) custom-call(bf16[32,96,128]{2,1,0:T(8,128)(2,1)} %bitcast.12, bf16[2,32,96,128]{3,2,1,0:T(8,128)(2,1)} %bitcast.10, s32[1,16]{1,0:T(1,128)} %bitcast.15, s32[1,16]{1,0:T(1,128)} %scored_ref.1, f32[1,96]{1,0:T(1,128)} %bitcast.16, f32[1,96]{1,0:T(1,128)} %bitcast.17, ...), custom_call_target="tpu_custom_call" | custom-call | tf_op jit(solution)/shard_map/pallas_call | solution.py:523
  121.1 0.0 copy-start
  121.1 1.2 copy-done
  122.4 0.0 copy-start.1
  122.4 2.7 %shard_map.104 = (f32[27,96,96]{2,1,0:T(8,128)}, f32[27,96,96]{2,1,0:T(8,128)}) custom-call(bf16[32,8,16,128]{3,2,1,0:T(8,128)(2,1)S(1)} %copy-done), custom_call_target="tpu_custom_call" | custom-call | tf_op jit(solution)/shard_map/pallas_call | solution.py:577
  125.0 0.0 copy-done.1
  125.0 0.9 copy.12
Async XLA Ops:
  121.1 1.2 copy-start
  122.4 2.7 %copy-start.1 = (bf16[32,96,128]{2,1,0:T(8,128)(2,1)S(1)}, bf16[32,96,128]{2,1,0:T(8,128)(2,1)}, u32[]{:S(2)}) copy-start(bf16[32,96,128]{2,1,0:T(8,128)(2,1)} %get-tuple-element.7) | copy-start | bytes 2359300
